TPU v7x, 256 devices: a whole 4x4x8 slice. The times are simulated.
256 devices in a mesh: ctx: 32 (over z_lo, y, x), exp: 8 (over z_hi, core).
Axes of the slice: x: 4, y: 4, z: 8 (z_hi: 4, z_lo: 2; z = z_hi * 2 + z_lo), core: 2. Of those that a mesh axis runs over, the one named last changes fastest.
Arguments:
- tokens: bfloat16 [4096, 2880], P('ctx'), may hold values from -6 to 6
- cotangent: bfloat16 [4096, 2880], P('ctx'), may hold values from -6 to 6
- expert_ids: int32 [4096, 4], P('ctx'), may hold values from 0 to 31, all different within a row; in each aligned block of 128 rows (0 to 127, 128 to 255, ...) at most 20 rows name the same one
- combine_weights: float32 [4096, 4], P('ctx'), may hold values from 0.05 to 1
- w_query: bfloat16 [2880, 2048], P('ctx', 'exp'), may hold values from -0.109375 to 0.109375
- key_value_weight: bfloat16 [2880, 1024], P('ctx', 'exp'), may hold values from -0.109375 to 0.109375
- w_output: bfloat16 [2048, 2880], P('exp', 'ctx'), may hold values from -0.125 to 0.125
- w_gate: bfloat16 [32, 2880, 2048], P('ctx', None, 'exp'), may hold values from -0.109375 to 0.109375
- w_up: bfloat16 [32, 2880, 2048], P('ctx', None, 'exp'), may hold values from -0.109375 to 0.109375
- w_down: bfloat16 [32, 2048, 2880], P('ctx', 'exp'), may hold values from -0.125 to 0.125
Outputs:
- block_out: bfloat16 [4096, 2880], P('ctx')
- grad_tokens: bfloat16 [4096, 2880], P('ctx')
- grad_query: bfloat16 [2880, 2048], P('ctx', 'exp')
- grad_keyval: bfloat16 [2880, 1024], P('ctx', 'exp')
- grad_output: bfloat16 [2048, 2880], P('exp', 'ctx')
- grad_gate: bfloat16 [32, 2880, 2048], P('ctx', None, 'exp')
- grad_up: bfloat16 [32, 2880, 2048], P('ctx', None, 'exp')
- grad_down: bfloat16 [32, 2048, 2880], P('ctx', 'exp')
Inputs may be any that keep to these rules, and one draw needn't show every extreme that they name: `expert_ids`: each row names 4 different experts. Within the 128 rows of one context block no expert is named more than 20 times, and in some block one expert is named exactly 20 times.
All inputs are finite; a program needn't handle non-finite values.
Results may differ from a plain program's by a relative error of at most 0.029.
Values may be sent and summed in bfloat16 or wider, within the bound.
A program may use at most 128 MiB of HBM per device.

v0:
```python
import jax
import jax.numpy as jnp
from jax import lax
from jax.sharding import PartitionSpec as P

QUERY_HEADS = 32
KEY_VALUE_HEADS = 8
HEAD_SIZE = 64
WINDOW = 128


EPSILON = 1e-05
GLU_ALPHA = 1.702


def shifted(shard, axis, by):
    size = lax.axis_size(axis)
    pairs = [(i, i + by) for i in range(size) if 0 <= i + by < size]
    return lax.ppermute(shard, axis, pairs)


def rms_norm(values):
    inv_rms = lax.rsqrt(jnp.mean(values * values, axis=-1, keepdims=True) + EPSILON)
    return (values * inv_rms, inv_rms)


def rms_back(values, inv_rms, grad_in):
    inner_mean = jnp.mean(grad_in * values, axis=-1, keepdims=True)
    return inv_rms * grad_in - values * (inv_rms * inv_rms * inv_rms) * inner_mean


def rounded(values):
    return lax.optimization_barrier(values.astype(jnp.bfloat16)).astype(jnp.float32)


def band_valid(row_count, band_width, block_idx):
    query_pos = block_idx * row_count + jnp.arange(row_count)[:, None]
    key_pos = block_idx * row_count - band_width + jnp.arange(band_width + row_count)[None, :]
    return (key_pos <= query_pos) & (key_pos > query_pos - band_width) & (key_pos >= 0)


def attend(query_matrix, key_value, valid_mask):
    key_rows = key_value[:, :, 0]
    value_rows = key_value[:, :, 1]
    scores = (
        jnp.einsum("tgjd,sgd->gjts", query_matrix, key_rows, preferred_element_type=jnp.float32)
        * 0.125
    )
    weights = jnp.where(valid_mask, jnp.exp(scores), 0.0)
    probability_single = weights / jnp.sum(weights, axis=-1, keepdims=True)
    probability_half = probability_single.astype(jnp.bfloat16)
    attended = jnp.einsum(
        "gjts,sgd->tgjd", probability_half, value_rows, preferred_element_type=jnp.float32
    )
    return (attended.astype(jnp.bfloat16), probability_single, probability_half)


def attention_backward(query_matrix, key_value, probability_single, probability_half, grad_out):
    key_rows = key_value[:, :, 0]
    value_rows = key_value[:, :, 1]
    grad_prob = jnp.einsum(
        "tgjd,sgd->gjts", grad_out, value_rows, preferred_element_type=jnp.float32
    )
    grad_value = jnp.einsum(
        "gjts,tgjd->sgd", probability_half, grad_out, preferred_element_type=jnp.float32
    )
    grad_score = (
        probability_single
        * (grad_prob - jnp.sum(grad_prob * probability_single, axis=-1, keepdims=True))
        * 0.125
    ).astype(jnp.bfloat16)
    query_gradients = jnp.einsum(
        "gjts,sgd->tgjd", grad_score, key_rows, preferred_element_type=jnp.float32
    )
    grad_key = jnp.einsum(
        "gjts,tgjd->sgd", grad_score, query_matrix, preferred_element_type=jnp.float32
    )
    return (query_gradients, jnp.stack([grad_key, grad_value], axis=2))


def place_routes(flat_ids, expert_count, capacity):
    one_hot = (flat_ids[:, None] == jnp.arange(expert_count)[None, :]).astype(jnp.int32)
    earlier = jnp.cumsum(one_hot, axis=0) - one_hot
    return flat_ids * capacity + jnp.sum(earlier * one_hot, axis=1)


def pick_rows(returned, route_table):
    feature_count = returned.shape[-1]
    flat_slots = returned.reshape(-1, feature_count)
    return jnp.einsum("tks,sd->tkd", route_table, flat_slots, preferred_element_type=jnp.float32)


def sum_heads(values):
    return lax.psum(values.astype(jnp.bfloat16), "exp").astype(jnp.float32)


def over_experts(buffer):
    return lax.all_to_all(buffer, "ctx", split_axis=0, concat_axis=0, tiled=True)


def back_from_experts(buffer):
    return lax.all_to_all(buffer, "ctx", split_axis=0, concat_axis=0, tiled=True)


def body(
    tokens,
    cotangent,
    expert_ids,
    combine_weights,
    w_query,
    key_value_weight,
    w_output,
    w_gate,
    w_up,
    w_down,
):
    row_count, model_width = tokens.shape
    top_count = expert_ids.shape[1]
    ctx_count = lax.axis_size("ctx")
    ctx_block = lax.axis_index("ctx")
    capacity = row_count * top_count * 5 // (4 * ctx_count)
    kv_heads = key_value_weight.shape[1] // (2 * HEAD_SIZE)
    query_head_group = QUERY_HEADS // KEY_VALUE_HEADS
    tokens_f32 = tokens.astype(jnp.float32)
    normed_f32, token_scale = rms_norm(tokens_f32)
    normed = normed_f32.astype(jnp.bfloat16)
    full_query, full_keyval, full_output = (
        lax.all_gather(w_query, "ctx", axis=0, tiled=True),
        lax.all_gather(key_value_weight, "ctx", axis=0, tiled=True),
        lax.all_gather(w_output, "ctx", axis=1, tiled=True),
    )
    query_matrix = jnp.dot(normed, full_query, preferred_element_type=jnp.float32).astype(
        jnp.bfloat16
    )
    key_value = jnp.dot(normed, full_keyval, preferred_element_type=jnp.float32).astype(
        jnp.bfloat16
    )
    prev_rim = shifted(key_value, "ctx", 1)
    query_heads = query_matrix.reshape(row_count, kv_heads, query_head_group, HEAD_SIZE)
    banded_key_span = jnp.concatenate([prev_rim, key_value], axis=0).reshape(
        WINDOW + row_count, kv_heads, 2, HEAD_SIZE
    )
    valid_mask = band_valid(row_count, WINDOW, ctx_block)
    attended, probability_single, probability_half = attend(
        query_heads, banded_key_span, valid_mask
    )
    attended_flat = attended.reshape(row_count, -1)
    head_part = jnp.dot(attended_flat, full_output, preferred_element_type=jnp.float32)
    residual = (tokens_f32 + sum_heads(head_part)).astype(jnp.bfloat16)
    moe_f32, resid_scale = rms_norm(residual.astype(jnp.float32))
    moe_input = moe_f32.astype(jnp.bfloat16)
    residual_f32 = residual.astype(jnp.float32)
    slot_count = ctx_count * capacity
    target = place_routes(expert_ids.reshape(-1), ctx_count, capacity)
    route_table = (
        (target[:, None] == jnp.arange(slot_count)[None, :])
        .astype(jnp.bfloat16)
        .reshape(row_count, top_count, slot_count)
    )
    slot_token = jnp.sum(route_table, axis=1)
    outgoing = jnp.dot(slot_token.T, moe_input, preferred_element_type=jnp.float32).astype(
        jnp.bfloat16
    )
    incoming = over_experts(outgoing.reshape(ctx_count, capacity, model_width))
    expert_rows = incoming.reshape(-1, model_width)
    gate_pre = jnp.dot(expert_rows, w_gate[0], preferred_element_type=jnp.float32)
    up_pre = jnp.dot(expert_rows, w_up[0], preferred_element_type=jnp.float32)
    gate_sig = jax.nn.sigmoid(GLU_ALPHA * gate_pre)
    gate_glu = gate_pre * gate_sig
    activated = (gate_glu * (up_pre + 1.0)).astype(jnp.bfloat16)
    down_part = (
        jnp.dot(activated, w_down[0], preferred_element_type=jnp.float32)
        .astype(jnp.bfloat16)
        .reshape(ctx_count, capacity, model_width)
    )
    route_scale = combine_weights[:, :, None]
    returned = back_from_experts(down_part)
    moe_total = sum_heads(jnp.sum(pick_rows(returned, route_table) * route_scale, axis=1))
    block_out = (residual_f32 + moe_total).astype(jnp.bfloat16)
    cot_f32 = cotangent.astype(jnp.float32)
    grad_rows = (route_scale * cot_f32[:, None, :]).astype(jnp.bfloat16)
    grad_sent = jnp.einsum(
        "tks,tkd->sd", route_table, grad_rows, preferred_element_type=jnp.float32
    ).astype(jnp.bfloat16)
    grad_expert = over_experts(grad_sent.reshape(ctx_count, capacity, model_width)).reshape(
        -1, model_width
    )
    grad_act = jnp.dot(grad_expert, w_down[0].T, preferred_element_type=jnp.float32)
    grad_gate_pre = (
        grad_act * (up_pre + 1.0) * (gate_sig + GLU_ALPHA * gate_glu * (1.0 - gate_sig))
    ).astype(jnp.bfloat16)
    grad_up_pre = (grad_act * gate_glu).astype(jnp.bfloat16)
    grad_down = jnp.dot(activated.T, grad_expert, preferred_element_type=jnp.float32).astype(
        jnp.bfloat16
    )[None]
    grad_gate = jnp.dot(expert_rows.T, grad_gate_pre, preferred_element_type=jnp.float32).astype(
        jnp.bfloat16
    )[None]
    grad_up = jnp.dot(expert_rows.T, grad_up_pre, preferred_element_type=jnp.float32).astype(
        jnp.bfloat16
    )[None]
    input_part = jnp.dot(grad_gate_pre, w_gate[0].T, preferred_element_type=jnp.float32) + jnp.dot(
        grad_up_pre, w_up[0].T, preferred_element_type=jnp.float32
    )
    input_part = input_part.astype(jnp.bfloat16).reshape(ctx_count, capacity, model_width)
    grad_returned = back_from_experts(input_part)
    grad_normed = sum_heads(jnp.sum(pick_rows(grad_returned, route_table), axis=1))
    grad_resid = cot_f32 + rms_back(residual_f32, resid_scale, grad_normed)
    grad_resid_bf = grad_resid.astype(jnp.bfloat16)
    attended_gradient = jnp.dot(
        grad_resid_bf, full_output.T, preferred_element_type=jnp.float32
    ).astype(jnp.bfloat16)
    query_gradients, key_value_gradients = attention_backward(
        query_heads,
        banded_key_span,
        probability_single,
        probability_half,
        attended_gradient.reshape(row_count, kv_heads, query_head_group, HEAD_SIZE),
    )
    rim_grad = shifted(key_value_gradients[:WINDOW].astype(jnp.bfloat16), "ctx", -1).astype(
        jnp.float32
    )
    local_gradient = key_value_gradients[WINDOW:].at[row_count - WINDOW :].add(rim_grad)
    key_value_grad = local_gradient.reshape(row_count, -1).astype(jnp.bfloat16)
    query_grad = query_gradients.reshape(row_count, -1).astype(jnp.bfloat16)
    grad_normed_in = sum_heads(
        jnp.dot(query_grad, full_query.T, preferred_element_type=jnp.float32)
        + jnp.dot(key_value_grad, full_keyval.T, preferred_element_type=jnp.float32)
    )
    grad_tokens = (grad_resid + rms_back(tokens_f32, token_scale, grad_normed_in)).astype(
        jnp.bfloat16
    )
    terms = (
        rounded(jnp.dot(normed.T, query_grad, preferred_element_type=jnp.float32)),
        rounded(jnp.dot(normed.T, key_value_grad, preferred_element_type=jnp.float32)),
        rounded(jnp.dot(attended_flat.T, grad_resid_bf, preferred_element_type=jnp.float32)),
    )
    sum_query, sum_keyval, sum_output = (
        lax.psum_scatter(
            terms[0].astype(jnp.bfloat16), "ctx", scatter_dimension=0, tiled=True
        ).astype(jnp.float32),
        lax.psum_scatter(
            terms[1].astype(jnp.bfloat16), "ctx", scatter_dimension=0, tiled=True
        ).astype(jnp.float32),
        lax.psum_scatter(
            terms[2].astype(jnp.bfloat16), "ctx", scatter_dimension=1, tiled=True
        ).astype(jnp.float32),
    )
    return (
        block_out,
        grad_tokens,
        sum_query.astype(jnp.bfloat16),
        sum_keyval.astype(jnp.bfloat16),
        sum_output.astype(jnp.bfloat16),
        grad_gate,
        grad_up,
        grad_down,
    )


def solution(mesh):
    in_specs = (
        P("ctx", None),
        P("ctx", None),
        P("ctx", None),
        P("ctx", None),
        P("ctx", "exp"),
        P("ctx", "exp"),
        P("exp", "ctx"),
        P("ctx", None, "exp"),
        P("ctx", None, "exp"),
        P("ctx", "exp", None),
    )
    out_specs = (
        P("ctx", None),
        P("ctx", None),
        P("ctx", "exp"),
        P("ctx", "exp"),
        P("exp", "ctx"),
        P("ctx", None, "exp"),
        P("ctx", None, "exp"),
        P("ctx", "exp", None),
    )
    return jax.shard_map(body, mesh=mesh, in_specs=in_specs, out_specs=out_specs, check_vma=False)
```

profile of v0, /device:TPU:82, one launch (start us, length us, event | category | flops | bytes accessed | tf_op | source)
XLA Modules:
  0.0 897.1 jit_solution(17111580672626592761)
XLA Ops:
  22.2 6.5 reshape.269
  28.7 8.9 all-to-all-start.2
  38.5 124.4 %all-gather = bf16[32,90,128]{2,1,0:T(8,128)(2,1)} all-gather(bf16[1,90,128]{2,1,0:T(8,128)(2,1)S(1)} %bitcast.179), channel_id=1, replica_groups=mesh['ctx'=32,'exp'=8] {'ctx'}, dimensions={0}, use_global_device_ids=true | all-gather | bytes 760320 | tf_op jit(solution)/shard_map/all_gather | solution.py:129
  172.5 10.1 %all-gather.6.cloned.1.call-done = bf16[32,90,256]{2,1,0:T(8,128)(2,1)} async-done(((bf16[1,90,256]{2,1,0:T(8,128)(2,1)}), bf16[32,90,256]{2,1,0:T(8,128)(2,1)}) %all-gather.6.cloned.1.call-update) | async-done | bytes 1474576 | tf_op jit(solution)/shard_map/all_gather | solution.py:128
  187.8 150.4 %all-gather.8.cloned.1.call-done = bf16[32,90,256]{2,1,0:T(8,128)(2,1)} async-done(((bf16[1,90,256]{2,1,0:T(8,128)(2,1)}), bf16[32,90,256]{2,1,0:T(8,128)(2,1)}) %all-gather.8.cloned.1.call-update) | async-done | bytes 1474576 | tf_op jit(solution)/shard_map/all_gather | solution.py:130
  344.8 81.4 %all-reduce.12.cloned.1.call-done = bf16[128,2880]{0,1:T(8,128)(2,1)} async-done(((bf16[128,2880]{0,1:T(8,128)(2,1)}), bf16[128,2880]{0,1:T(8,128)(2,1)}) %all-reduce.12.cloned.1.call-update) | async-done | bytes 737296 | tf_op jit(solution)/shard_map/psum | solution.py:94
  436.9 6.5 reshape.265
  443.4 7.4 all-to-all-start
  450.8 6.5 reshape.270
  457.3 51.7 %all-to-all-done = bf16[32,20,2880]{2,1,0:T(8,128)(2,1)} async-done(((bf16[32,20,2880]{2,1,0:T(8,128)(2,1)}), bf16[32,20,2880]{2,1,0:T(8,128)(2,1)}, u32[]{:S(2)}, u32[]{:S(2)}) %all-to-all-start) | async-done | bytes 3686432 | tf_op jit(solution)/shard_map/all_to_all | solution.py:98
  534.1 6.5 reshape.271
  540.6 10.1 %all-to-all-start.3 = ((bf16[32,20,2880]{2,1,0:T(8,128)(2,1)}), bf16[32,20,2880]{2,1,0:T(8,128)(2,1)}, u32[]{:S(2)}, u32[]{:S(2)}) async-start(bf16[32,20,2880]{2,1,0:T(8,128)(2,1)} %reshape.271), calls=%async_computation.3 | async-start | bytes 9043968 | tf_op jit(solution)/shard_map/all_to_all | solution.py:102
  560.1 6.4 reshape.267
  566.5 52.8 %all-to-all-done.3 = bf16[32,20,2880]{2,1,0:T(8,128)(2,1)} async-done(((bf16[32,20,2880]{2,1,0:T(8,128)(2,1)}), bf16[32,20,2880]{2,1,0:T(8,128)(2,1)}, u32[]{:S(2)}, u32[]{:S(2)}) %all-to-all-start.3) | async-done | bytes 3686432 | tf_op jit(solution)/shard_map/all_to_all | solution.py:102
  619.3 9.3 %all-to-all-start.1 = ((bf16[32,20,2880]{2,1,0:T(8,128)(2,1)}), bf16[32,20,2880]{2,1,0:T(8,128)(2,1)}, u32[]{:S(2)}, u32[]{:S(2)}) async-start(bf16[32,20,2880]{2,1,0:T(8,128)(2,1)} %reshape.267), calls=%async_computation.1 | async-start | bytes 9043968 | tf_op jit(solution)/shard_map/all_to_all | solution.py:102
  634.7 6.5 reshape.272
  641.2 6.6 fusion.12
  652.5 38.2 %all-to-all-done.1 = bf16[32,20,2880]{2,1,0:T(8,128)(2,1)} async-done(((bf16[32,20,2880]{2,1,0:T(8,128)(2,1)}), bf16[32,20,2880]{2,1,0:T(8,128)(2,1)}, u32[]{:S(2)}, u32[]{:S(2)}) %all-to-all-start.1) | async-done | bytes 3686432 | tf_op jit(solution)/shard_map/all_to_all | solution.py:102
  690.7 6.5 reshape.268
  697.2 6.7 multiply_reduce_fusion
  704.0 18.5 %all-reduce.14.cloned.1.call-done = bf16[128,2880]{0,1:T(8,128)(2,1)} async-done(((bf16[128,2880]{0,1:T(8,128)(2,1)}), bf16[128,2880]{0,1:T(8,128)(2,1)}) %all-reduce.14.cloned.1.call-update) | async-done | bytes 737296 | tf_op jit(solution)/shard_map/psum | solution.py:94
  739.1 95.0 %fusion.78 = (bf16[96,256]{1,0:T(8,128)(2,1)S(1)}, bf16[96,128]{1,0:T(8,128)(2,1)S(1)}, bf16[256,96]{0,1:T(8,128)(2,1)S(1)}) fusion(bf16[2880,256]{1,0:T(8,128)(2,1)S(1)} %convolution_convert_fusion.6, bf16[2880,128]{1,0:T(8,128)(2,1)} %convolution_convert_fusion.7, bf16[256,2880]{0,1:T(8,128)(2,1)} %convolution_convert_fusion.5), kind=kCustom, calls=%all-reduce-scatter.3 | all-reduce-scatter fusion | flops 1966081 | bytes 3810304
  838.4 11.3 %collective-permute-start.5 = (bf16[90,128]{1,0:T(8,128)(2,1)S(1)}, bf16[90,128]{1,0:T(8,128)(2,1)S(1)}, u32[]{:S(2)}, u32[]{:S(2)}) collective-permute-start(bf16[90,128]{1,0:T(8,128)(2,1)S(1)} %slice.57), channel_id=1, source_target_pairs={{0,16},{8,24},{16,32},{24,40},{32,48},{40,56},{48,64},{56,72},{64,... | collective-permute-start | bytes 69128
  863.5 11.3 %collective-permute-start.7 = (bf16[256,90]{0,1:T(8,128)(2,1)S(1)}, bf16[256,90]{0,1:T(8,128)(2,1)S(1)}, u32[]{:S(2)}, u32[]{:S(2)}) collective-permute-start(bf16[256,90]{0,1:T(8,128)(2,1)S(1)} %slice.58), channel_id=1, source_target_pairs={{0,16},{8,24},{16,32},{24,40},{32,48},{40,56},{48,64},{56,72},{64,... | collective-permute-start | bytes 138248
  (178 shorter events, 142.2 us)
Async XLA Ops:
  7.2 513.6 %copy-start = (bf16[1,256,2880]{1,2,0:T(8,128)(2,1)S(1)}, bf16[1,256,2880]{1,2,0:T(8,128)(2,1)}, u32[]{:S(2)}) copy-start(bf16[1,256,2880]{1,2,0:T(8,128)(2,1)} %param.23) | copy-start | bytes 4423684
  7.2 175.3 %all-gather.6.cloned.1.call-start = ((), (), s32[]{:S(2)}) async-start(), calls=%async_computation.6 | async-start | bytes 1622016 | tf_op jit(solution)/shard_map/all_gather | solution.py:128
  28.7 414.7 %all-to-all-start.2 = ((bf16[32,20,2880]{2,1,0:T(8,128)(2,1)}), bf16[32,20,2880]{2,1,0:T(8,128)(2,1)}, u32[]{:S(2)}, u32[]{:S(2)}) async-start(bf16[32,20,2880]{2,1,0:T(8,128)(2,1)} %reshape.269), calls=%async_computation.2 | async-start | bytes 9043968 | tf_op jit(solution)/shard_map/all_to_all | solution.py:98
  37.6 126.6 %copy-start.2 = (bf16[128,2880]{0,1:T(8,128)(2,1)S(1)}, bf16[128,2880]{0,1:T(8,128)(2,1)}, u32[]{:S(2)}) copy-start(bf16[128,2880]{0,1:T(8,128)(2,1)} %param.14) | copy-start | bytes 2211844
  37.6 300.6 %all-gather.8.cloned.1.call-start = ((), (), s32[]{:S(2)}) async-start(), calls=%async_computation.7 | async-start | bytes 1622016 | tf_op jit(solution)/shard_map/all_gather | solution.py:130
  38.4 387.8 %all-reduce.12.cloned.1.call-start = ((), (), s32[]{:S(2)}) async-start(), calls=%async_computation.4 | async-start | bytes 1474560 | tf_op jit(solution)/shard_map/psum | solution.py:94
  165.6 6.7 collective-permute-start
  172.4 169.4 %copy-start.27 = (bf16[256,128]{0,1:T(8,128)(2,1)}, bf16[256,128]{0,1:T(8,128)(2,1)S(1)}, u32[]{:S(2)}) copy-start(bf16[256,128]{0,1:T(8,128)(2,1)S(1)} %copy.68) | copy-start | bytes 196612
  187.8 153.8 %copy-start.25 = (bf16[128,256]{0,1:T(8,128)(2,1)}, bf16[128,256]{0,1:T(8,128)(2,1)S(1)}, u32[]{:S(2)}) copy-start(bf16[128,256]{0,1:T(8,128)(2,1)S(1)} %copy.69) | copy-start | bytes 196612
  443.4 65.7 %all-to-all-start = ((bf16[32,20,2880]{2,1,0:T(8,128)(2,1)}), bf16[32,20,2880]{2,1,0:T(8,128)(2,1)}, u32[]{:S(2)}, u32[]{:S(2)}) async-start(bf16[32,20,2880]{2,1,0:T(8,128)(2,1)} %reshape.265), calls=%async_computation | async-start | bytes 9043968 | tf_op jit(solution)/shard_map/all_to_all | solution.py:98
  540.6 78.8 %all-to-all-start.3 = ((bf16[32,20,2880]{2,1,0:T(8,128)(2,1)}), bf16[32,20,2880]{2,1,0:T(8,128)(2,1)}, u32[]{:S(2)}, u32[]{:S(2)}) async-start(bf16[32,20,2880]{2,1,0:T(8,128)(2,1)} %reshape.271), calls=%async_computation.3 | async-start | bytes 9043968 | tf_op jit(solution)/shard_map/all_to_all | solution.py:102
  566.5 62.4 %copy-start.35 = (u32[256]{0:T(256)S(1)}, u32[256]{0:T(256)}, u32[]{:S(2)}) copy-start(u32[256]{0:T(256)} %constant.82) | copy-start | bytes 3076
  566.5 63.6 %copy-start.22 = (bf16[640,256]{1,0:T(8,128)(2,1)S(1)}, bf16[640,256]{1,0:T(8,128)(2,1)}, u32[]{:S(2)}) copy-start(bf16[640,256]{1,0:T(8,128)(2,1)} %copy-done.21) | copy-start | bytes 983044
  619.3 71.4 %all-to-all-start.1 = ((bf16[32,20,2880]{2,1,0:T(8,128)(2,1)}), bf16[32,20,2880]{2,1,0:T(8,128)(2,1)}, u32[]{:S(2)}, u32[]{:S(2)}) async-start(bf16[32,20,2880]{2,1,0:T(8,128)(2,1)} %reshape.267), calls=%async_computation.1 | async-start | bytes 9043968 | tf_op jit(solution)/shard_map/all_to_all | solution.py:102
  628.6 93.9 %all-reduce.14.cloned.1.call-start = ((), (), s32[]{:S(2)}) async-start(), calls=%async_computation.5 | async-start | bytes 1474560 | tf_op jit(solution)/shard_map/psum | solution.py:94
  647.9 237.5 %all-reduce.16.cloned.1.call-start = ((), (), s32[]{:S(2)}) async-start(), calls=%async_computation.8 | async-start | bytes 2949120 | tf_op jit(solution)/shard_map/psum | solution.py:94
  730.8 5.8 collective-permute-start.1
  739.1 110.7 %copy-start.20 = (bf16[640,256]{1,0:T(8,128)(2,1)S(1)}, bf16[640,256]{1,0:T(8,128)(2,1)}, u32[]{:S(2)}) copy-start(bf16[640,256]{1,0:T(8,128)(2,1)} %copy-done.19) | copy-start | bytes 983044
  834.1 42.6 %collective-permute-start.4 = (bf16[96,128]{1,0:T(8,128)(2,1)S(1)}, bf16[96,128]{1,0:T(8,128)(2,1)S(1)}, u32[]{:S(2)}, u32[]{:S(2)}) collective-permute-start(bf16[96,128]{1,0:T(8,128)(2,1)S(1)} %get-tuple-element.34), channel_id=1, source_target_pairs={{0,8},{8,16},{16,24},{24,32},{32,40},{40,48},{48,56},{56,64},{64,7... | collective-permute-start | bytes 73736
  838.4 36.4 %collective-permute-start.5 = (bf16[90,128]{1,0:T(8,128)(2,1)S(1)}, bf16[90,128]{1,0:T(8,128)(2,1)S(1)}, u32[]{:S(2)}, u32[]{:S(2)}) collective-permute-start(bf16[90,128]{1,0:T(8,128)(2,1)S(1)} %slice.57), channel_id=1, source_target_pairs={{0,16},{8,24},{16,32},{24,40},{32,48},{40,56},{48,64},{56,72},{64,... | collective-permute-start | bytes 69128
  854.6 28.6 %collective-permute-start.2 = (bf16[96,256]{1,0:T(8,128)(2,1)S(1)}, bf16[96,256]{1,0:T(8,128)(2,1)S(1)}, u32[]{:S(2)}, u32[]{:S(2)}) collective-permute-start(bf16[96,256]{1,0:T(8,128)(2,1)S(1)} %get-tuple-element.33), channel_id=1, source_target_pairs={{0,8},{8,16},{16,24},{24,32},{32,40},{40,48},{48,56},{56,64},{64,7... | collective-permute-start | bytes 147464
  858.1 25.6 %collective-permute-start.6 = (bf16[256,96]{0,1:T(8,128)(2,1)S(1)}, bf16[256,96]{0,1:T(8,128)(2,1)S(1)}, u32[]{:S(2)}, u32[]{:S(2)}) collective-permute-start(bf16[256,96]{0,1:T(8,128)(2,1)S(1)} %get-tuple-element.35), channel_id=1, source_target_pairs={{0,8},{8,16},{16,24},{24,32},{32,40},{40,48},{48,56},{56,64},{64,7... | collective-permute-start | bytes 147464
  863.5 20.2 %collective-permute-start.7 = (bf16[256,90]{0,1:T(8,128)(2,1)S(1)}, bf16[256,90]{0,1:T(8,128)(2,1)S(1)}, u32[]{:S(2)}, u32[]{:S(2)}) collective-permute-start(bf16[256,90]{0,1:T(8,128)(2,1)S(1)} %slice.58), channel_id=1, source_target_pairs={{0,16},{8,24},{16,32},{24,40},{32,48},{40,56},{48,64},{56,72},{64,... | collective-permute-start | bytes 138248
  874.8 8.4 collective-permute-start.3
  (30 other events, 176.5 us)
Sparse Core Ops, SparseCore 0:
  9.8 172.6 all-gather.5
  184.3 153.8 all-gather.7
  344.7 81.4 all-reduce.11
  648.0 74.3 all-reduce.13
  739.2 84.5 all-reduce.15
where the time goes:
time: 900 us; the launch traced here: 897 us
  waiting for transfers between devices  413 us (46%)
  blocking collectives  219 us (24%)
  local copies, waits for them, and re-layouts  95.2 us (11%)
  starting transfers between devices  80.3 us (9%)
  matrix products  61.4 us (7%)
  between operations  15.1 us (2%)
  other arithmetic  12.2 us (1%)
    all_gather x1, waiting for transfers between devices, body(): lax.all_gather(w_output, 'ctx', axis=1, tiled=True)  150 us
    all_gather x1, blocking collectives, body(): lax.all_gather(key_value_weight, 'ctx', axis=0, tiled=True)  124 us
    psum x3, waiting for transfers between devices, sum_heads(): return lax.psum(values.astype(jnp.bfloat16), 'exp').astype(jnp.float32)  99.9 us
    unnamed x1, blocking collectives  95 us
    all_to_all x2, waiting for transfers between devices, back_from_experts(): lax.all_to_all(buffer, 'ctx', split_axis=0, concat_axis=0, tiled=True)  91 us
    all_to_all x2, waiting for transfers between devices, over_experts(): lax.all_to_all(buffer, 'ctx', split_axis=0, concat_axis=0, tiled=True)  51.7 us
    unnamed x6, starting transfers between devices  37.7 us
    all_to_all x2, starting transfers between devices, back_from_experts(): lax.all_to_all(buffer, 'ctx', split_axis=0, concat_axis=0, tiled=True)  19.3 us
  transfers between devices with their start and end apart: 17, of which 10 were waited for; matrix products, arithmetic and copies ran while one was open for 24% of the time, Pallas kernels for 0%

commit v1 on v0

v1 whole, which is shorter than its diff:
```python
import functools

import jax
import jax.numpy as jnp
from jax import lax
from jax.experimental import pallas as pl
from jax.experimental.pallas import tpu as pltpu
from jax.sharding import PartitionSpec as P

CTX, EXP = "ctx", "exp"
SHARD = 90
PADDED = 96
HALF_LANES = 1920
MESH = pl.DeviceIdType.MESH
VMEM_BYTES = 60 * 2**20


def params(collective_id):
    return pltpu.CompilerParams(
        collective_id=collective_id, has_side_effects=True, vmem_limit_bytes=VMEM_BYTES
    )


def vmem_specs(count):
    return [pl.BlockSpec(memory_space=pltpu.VMEM)] * count


def place():
    c = lax.axis_index(CTX)
    return c, c // 16, (c // 4) % 4, c % 4


def greet(peers):
    barrier = pltpu.get_barrier_semaphore()
    for peer in peers:
        pl.semaphore_signal(barrier, inc=1, device_id=peer, device_id_type=MESH)
    pl.semaphore_wait(barrier, len(peers))


def gather_kernel(w_ref, out_ref, send, recv):
    c, z, y, x = place()
    e = lax.axis_index(EXP)

    def dev(zz, yy, xx):
        return (zz * 16 + ((yy + 4) % 4) * 4 + (xx + 4) % 4, e)

    def copy(n, src, dst, to):
        cp = pltpu.make_async_remote_copy(
            src_ref=src, dst_ref=dst, send_sem=send.at[n], recv_sem=recv.at[n],
            device_id=to, device_id_type=MESH,
        )
        cp.start()
        return cp

    greet([dev(1 - z, y, x), dev(z, y + 1, x), dev(z, y - 1, x), dev(z, y, x + 1), dev(z, y, x - 1)])
    rows = (pl.ds(0, 48), pl.ds(48, 48))
    copies = []
    first = []
    for h in range(2):
        first.append(copy(h, w_ref.at[rows[h]], out_ref.at[z, y, x, rows[h]], dev(1 - z, y, x)))
    out_ref[z, y, x] = w_ref[...]
    copies += first

    def view(h, phase, zsel, pos):
        along_x = (h == 0) == (phase == 1)
        if phase == 1:
            return out_ref.at[zsel, y, pos, rows[h]] if along_x else out_ref.at[zsel, pos, x, rows[h]]
        return out_ref.at[zsel, :, pos, rows[h]] if along_x else out_ref.at[zsel, pos, :, rows[h]]

    def ring(h, phase):
        along_x = (h == 0) == (phase == 1)
        me = x if along_x else y
        up = dev(z, y, x + 1) if along_x else dev(z, y + 1, x)
        down = dev(z, y, x - 1) if along_x else dev(z, y - 1, x)
        return me, (me + 3) % 4, (me + 1) % 4, up, down

    for phase in (1, 2):
        direct = []
        for h in range(2):
            for cp in first[h] if phase == 2 else (first[h],):
                cp.wait_recv()
            me, low, high, up, down = ring(h, phase)
            n = 2 + (phase - 1) * 8 + h * 4
            both = pl.ds(0, 2)
            direct.append((
                copy(n, view(h, phase, both, me), view(h, phase, both, me), up),
                copy(n + 1, view(h, phase, both, me), view(h, phase, both, me), down),
            ))
        later = []
        for h in range(2):
            me, low, high, up, down = ring(h, phase)
            n = 2 + (phase - 1) * 8 + h * 4
            direct[h][0].wait_recv()
            a = copy(n + 2, view(h, phase, 0, low), view(h, phase, 0, low), up)
            direct[h][1].wait_recv()
            b = copy(n + 3, view(h, phase, 1, high), view(h, phase, 1, high), down)
            later.append((a, b))
        for h in range(2):
            copies += [*direct[h], *later[h]]
        first = later
    for h in range(2):
        for cp in first[h]:
            cp.wait_recv()
    for cp in copies:
        cp.wait_send()


def gather_weights(shard):
    out = pl.pallas_call(
        gather_kernel,
        out_shape=jax.ShapeDtypeStruct((2, 4, 4, PADDED, 640), jnp.bfloat16),
        in_specs=vmem_specs(1),
        out_specs=vmem_specs(1)[0],
        scratch_shapes=[pltpu.SemaphoreType.DMA((18,)), pltpu.SemaphoreType.DMA((18,))],
        compiler_params=params(0),
        name="gather_weights",
    )(shard)
    return out.reshape(32 * PADDED, 640)


def f32(v):
    return v.astype(jnp.float32)


def bf(v):
    return v.astype(jnp.bfloat16)


def scatter_kernel(t_ref, out_ref, far, near, stage, acc1, far2, near2, stage2, acc2, last, send, recv):
    c, z, y, x = place()
    e = lax.axis_index(EXP)

    def dev(zz, yy, xx):
        return (zz * 16 + ((yy + 4) % 4) * 4 + (xx + 4) % 4, e)

    def copy(n, src, dst, to):
        cp = pltpu.make_async_remote_copy(
            src_ref=src, dst_ref=dst, send_sem=send.at[n], recv_sem=recv.at[n],
            device_id=to, device_id_type=MESH,
        )
        cp.start()
        return cp

    greet([dev(1 - z, y, x), dev(z, y + 1, x), dev(z, y - 1, x), dev(z, y, x + 1), dev(z, y, x - 1)])
    rows = (pl.ds(0, 48), pl.ds(48, 48))
    copies = []

    def ring(along_x):
        me = x if along_x else y
        up = dev(z, y, x + 1) if along_x else dev(z, y + 1, x)
        down = dev(z, y, x - 1) if along_x else dev(z, y - 1, x)
        return me, (me + 3) % 4, (me + 1) % 4, (me + 2) % 4, up, down

    def step(phase, source, far_ref, near_ref, stage_ref):
        started = []
        for h in range(2):
            me, low, high, across, up, down = ring((h == 1) == (phase == 1))
            n = (phase - 1) * 12 + h * 6
            started.append([
                copy(n, source(h, 0, across), far_ref.at[h, 0], up),
                copy(n + 1, source(h, 1, across), far_ref.at[h, 1], down),
                copy(n + 2, source(h, 1, high), near_ref.at[h, 0, 1], up),
                copy(n + 3, source(h, 0, low), near_ref.at[h, 1, 0], down),
            ])
        for h in range(2):
            me, low, high, across, up, down = ring((h == 1) == (phase == 1))
            n = (phase - 1) * 12 + h * 6
            started[h][0].wait_recv()
            stage_ref[h, 0] = bf(f32(source(h, 0, high)[...]) + f32(far_ref[h, 0]))
            started[h].append(copy(n + 4, stage_ref.at[h, 0], near_ref.at[h, 0, 0], up))
            started[h][1].wait_recv()
            stage_ref[h, 1] = bf(f32(source(h, 1, low)[...]) + f32(far_ref[h, 1]))
            started[h].append(copy(n + 5, stage_ref.at[h, 1], near_ref.at[h, 1, 1], down))
        return started

    def first_source(h, zsel, pos):
        return t_ref.at[zsel, pos, :, rows[h]] if h == 0 else t_ref.at[zsel, :, pos, rows[h]]

    started = step(1, first_source, far, near, stage)
    for h in range(2):
        me = ring(h == 1)[0]
        for i in (2, 3, 4, 5):
            started[h][i].wait_recv()
        for zz in range(2):
            acc1[h, zz] = bf(f32(first_source(h, zz, me)[...]) + f32(near[h, 0, zz]) + f32(near[h, 1, zz]))
        copies += started[h]

    def second_source(h, zsel, pos):
        return acc1.at[h, zsel, pos]

    started = step(2, second_source, far2, near2, stage2)
    final = []
    for h in range(2):
        me = ring(h == 0)[0]
        for i in (2, 3, 4, 5):
            started[h][i].wait_recv()
        for zz in range(2):
            acc2[h, zz] = bf(f32(second_source(h, zz, me)[...]) + f32(near2[h, 0, zz]) + f32(near2[h, 1, zz]))
        copies += started[h]
        final.append(copy(24 + h, acc2.at[h, 1 - z], last.at[h], dev(1 - z, y, x)))
    for h in range(2):
        final[h].wait_recv()
        out_ref[rows[h], :] = bf(f32(acc2[h, z]) + f32(last[h]))
    for cp in copies + final:
        cp.wait_send()


def scatter_sums(terms):
    b = jnp.bfloat16
    return pl.pallas_call(
        scatter_kernel,
        out_shape=jax.ShapeDtypeStruct((PADDED, 640), b),
        in_specs=vmem_specs(1),
        out_specs=vmem_specs(1)[0],
        scratch_shapes=[
            pltpu.VMEM((2, 2, 4, 48, 640), b),
            pltpu.VMEM((2, 2, 2, 4, 48, 640), b),
            pltpu.VMEM((2, 2, 4, 48, 640), b),
            pltpu.VMEM((2, 2, 4, 48, 640), b),
            pltpu.VMEM((2, 2, 48, 640), b),
            pltpu.VMEM((2, 2, 2, 48, 640), b),
            pltpu.VMEM((2, 2, 48, 640), b),
            pltpu.VMEM((2, 2, 48, 640), b),
            pltpu.VMEM((2, 48, 640), b),
            pltpu.SemaphoreType.DMA((26,)),
            pltpu.SemaphoreType.DMA((26,)),
        ],
        compiler_params=params(1),
        name="scatter_sums",
    )(terms.reshape(2, 4, 4, PADDED, 640))


def shifted_by(z, y, x, i, sign):
    dz, dy, dx = i // 16, (i // 4) % 4, i % 4
    return ((z + dz) % 2) * 16 + ((y + sign * dy + 4) % 4) * 4 + (x + sign * dx + 4) % 4


def greet_all(c, z, y, x, e, partner):
    barrier = pltpu.get_barrier_semaphore()

    def hello(i, carry):
        pl.semaphore_signal(
            barrier, inc=1, device_id=(shifted_by(z, y, x, i, 1), e), device_id_type=MESH
        )
        return carry

    lax.fori_loop(1, 32, hello, 0)
    pl.semaphore_signal(barrier, inc=1, device_id=partner, device_id_type=MESH)
    pl.semaphore_wait(barrier, 32)


def dispatch_kernel(arrays, *refs):
    ins, outs = refs[:arrays], refs[arrays : 2 * arrays]
    send, recv, send2, recv2 = refs[2 * arrays :]
    c, z, y, x = place()
    e = lax.axis_index(EXP)
    k = e % 2
    partner = (c, e + 1 - 2 * k)
    greet_all(c, z, y, x, e, partner)
    for a in range(arrays):
        outs[a][k, c] = ins[a][k, c]

    def out_copy(a, i):
        to = shifted_by(z, y, x, i, 1)
        return pltpu.make_async_remote_copy(
            src_ref=ins[a].at[k, to], dst_ref=outs[a].at[k, c],
            send_sem=send.at[a, i], recv_sem=recv.at[a, i],
            device_id=(to, e), device_id_type=MESH,
        )

    def across(a, i):
        source = shifted_by(z, y, x, i, -1)
        return pltpu.make_async_remote_copy(
            src_ref=outs[a].at[k, source], dst_ref=outs[a].at[k, source],
            send_sem=send2.at[a, i], recv_sem=recv2.at[a, i],
            device_id=partner, device_id_type=MESH,
        )

    for a in range(arrays):
        lax.fori_loop(1, 32, lambda i, t, a=a: (out_copy(a, i).start(), t)[1], 0)
    for a in range(arrays):
        across(a, 0).start()

    def arrived(a, i, t):
        out_copy(a, i).wait_recv()
        across(a, i).start()
        return t

    for a in range(arrays):
        lax.fori_loop(1, 32, lambda i, t, a=a: arrived(a, i, t), 0)

    def ended(a, i, t):
        across(a, i).wait()
        return t

    for a in range(arrays):
        lax.fori_loop(0, 32, lambda i, t, a=a: ended(a, i, t), 0)
        lax.fori_loop(1, 32, lambda i, t, a=a: (out_copy(a, i).wait_send(), t)[1], 0)


def dispatch(*packed):
    count = len(packed)
    shape = jax.ShapeDtypeStruct((2, 32, 16, HALF_LANES), jnp.bfloat16)
    return pl.pallas_call(
        functools.partial(dispatch_kernel, count),
        out_shape=[shape] * count,
        in_specs=vmem_specs(count),
        out_specs=vmem_specs(count),
        scratch_shapes=[pltpu.SemaphoreType.DMA((count, 32))] * 4,
        compiler_params=params(2),
        name="dispatch_rows",
    )(*packed)


def giveback_kernel(arrays, *refs):
    ins, outs = refs[:arrays], refs[arrays : 2 * arrays]
    other, stage, send, recv, send2, recv2 = refs[2 * arrays :]
    c, z, y, x = place()
    e = lax.axis_index(EXP)
    k = e % 2
    partner = (c, e + 1 - 2 * k)
    greet_all(c, z, y, x, e, partner)

    def across(a, i):
        to = shifted_by(z, y, x, i, 1)
        return pltpu.make_async_remote_copy(
            src_ref=ins[a].at[1 - k, to], dst_ref=other.at[a, to],
            send_sem=send2.at[a, i], recv_sem=recv2.at[a, i],
            device_id=partner, device_id_type=MESH,
        )

    def home(a, i):
        to = shifted_by(z, y, x, i, 1)
        return pltpu.make_async_remote_copy(
            src_ref=stage.at[a, to], dst_ref=outs[a].at[c],
            send_sem=send.at[a, i], recv_sem=recv.at[a, i],
            device_id=(to, e), device_id_type=MESH,
        )

    for a in range(arrays):
        lax.fori_loop(1, 32, lambda i, t, a=a: (across(a, i).start(), t)[1], 0)
        across(a, 0).start()

    def added(a, i, t):
        across(a, i).wait_recv()
        to = shifted_by(z, y, x, i, 1)
        stage[a, to] = bf(f32(ins[a][k, to]) + f32(other[a, to]))
        home(a, i).start()
        return t

    for a in range(arrays):
        lax.fori_loop(1, 32, lambda i, t, a=a: added(a, i, t), 0)
        across(a, 0).wait_recv()
        outs[a][c] = bf(f32(ins[a][k, c]) + f32(other[a, c]))
    for a in range(arrays):
        lax.fori_loop(1, 32, lambda i, t, a=a: (home(a, i).wait(), t)[1], 0)
        lax.fori_loop(0, 32, lambda i, t, a=a: (across(a, i).wait_send(), t)[1], 0)


def giveback(*parts):
    count = len(parts)
    b = jnp.bfloat16
    return pl.pallas_call(
        functools.partial(giveback_kernel, count),
        out_shape=[jax.ShapeDtypeStruct((32, 16, HALF_LANES), b)] * count,
        in_specs=vmem_specs(count),
        out_specs=vmem_specs(count),
        scratch_shapes=[
            pltpu.VMEM((count, 32, 16, HALF_LANES), b),
            pltpu.VMEM((count, 32, 16, HALF_LANES), b),
        ] + [pltpu.SemaphoreType.DMA((count, 32))] * 4,
        compiler_params=params(3),
        name="return_rows",
    )(*parts)


def sum_kernel(post, extra_in, extra_out, *refs):
    part = refs[0]
    ins = refs[1 : 1 + extra_in]
    out = refs[1 + extra_in]
    outs = refs[2 + extra_in : 2 + extra_in + extra_out]
    mate, stage, got, send, recv = refs[2 + extra_in + extra_out :]
    c = lax.axis_index(CTX)
    e = lax.axis_index(EXP)
    h, k = e // 2, e % 2
    partner = (c, e + 1 - 2 * k)

    def peer(d):
        return (c, ((h + d) % 4) * 2 + k)

    greet([partner, peer(1), peer(2), peer(3)])

    def rows(core, block):
        return pl.ds(pl.multiple_of(core * 64 + block * 16, 16), 16)

    def copy(n, src, dst, to):
        cp = pltpu.make_async_remote_copy(
            src_ref=src, dst_ref=dst, send_sem=send.at[n], recv_sem=recv.at[n],
            device_id=to, device_id_type=MESH,
        )
        cp.start()
        return cp

    order = (2, 1, 3, 0)
    copies, pair, far = [], {}, {}
    for d in order:
        b = (h + d) % 4
        pair[d] = copy(d, part.at[rows(1 - k, b)], mate.at[b], partner)
    for d in order:
        b = (h + d) % 4
        pair[d].wait_recv()
        both = f32(part[rows(k, b), :]) + f32(mate[b])
        if d:
            stage[d - 1] = bf(both)
            far[d] = copy(4 + d, stage.at[d - 1], got.at[d - 1], peer(d))
    total = both
    for d in (1, 3, 2):
        far[d].wait_recv()
        total = total + f32(got[d - 1])
    mine = rows(k, h)
    out[mine, :] = post(total, mine, *ins, *outs)
    spread = {d: copy(8 + d, out.at[mine], out.at[mine], peer(d)) for d in (2, 1, 3)}
    passed = [copy(12, out.at[mine], out.at[mine], partner)]
    for d in (1, 3, 2):
        spread[d].wait_recv()
        theirs = rows(k, (h - d + 4) % 4)
        passed.append(copy(12 + d, out.at[theirs], out.at[theirs], partner))
    for cp in passed:
        cp.wait_recv()
    for cp in [*pair.values(), *far.values(), *spread.values(), *passed]:
        cp.wait_send()


def sum_heads(part, post, ins, collective_id, extra_outs=(), name="sum_heads"):
    b = jnp.bfloat16
    width = part.shape[1]
    res = pl.pallas_call(
        functools.partial(sum_kernel, post, len(ins), len(extra_outs)),
        out_shape=[jax.ShapeDtypeStruct((128, width), b), *extra_outs],
        in_specs=vmem_specs(1 + len(ins)),
        out_specs=vmem_specs(1 + len(extra_outs)),
        scratch_shapes=[
            pltpu.VMEM((4, 16, width), b),
            pltpu.VMEM((3, 16, width), b),
            pltpu.VMEM((3, 16, width), b),
            pltpu.SemaphoreType.DMA((16,)),
            pltpu.SemaphoreType.DMA((16,)),
        ],
        compiler_params=params(collective_id),
        name=name,
    )(part, *ins)
    return res


EPSILON = 1e-05
GLU_ALPHA = 1.702
QUERY_HEADS = 32
KEY_VALUE_HEADS = 8
HEAD_SIZE = 64
WINDOW = 128
MODEL = 2880
GROUP = QUERY_HEADS // KEY_VALUE_HEADS


def dot(a, b):
    return jnp.dot(a, b, preferred_element_type=jnp.float32)


def dot_tn(a, b):
    return lax.dot_general(a, b, (((0,), (0,)), ((), ())), preferred_element_type=jnp.float32)


def dot_nt(a, b):
    return lax.dot_general(a, b, (((1,), (1,)), ((), ())), preferred_element_type=jnp.float32)


def inverse_rms(values):
    return lax.rsqrt(jnp.mean(values * values, axis=-1, keepdims=True) + EPSILON)


def rms_back(values, inv_rms, grad_in):
    inner_mean = jnp.mean(grad_in * values, axis=-1, keepdims=True)
    return inv_rms * grad_in - values * (inv_rms * inv_rms * inv_rms) * inner_mean


def shifted(shard, by):
    size = lax.axis_size(CTX)
    pairs = [(i, i + by) for i in range(size) if 0 <= i + by < size]
    return lax.ppermute(shard, CTX, pairs)


def pad_features(v):
    return jnp.pad(v.reshape(-1, 32, SHARD), ((0, 0), (0, 0), (0, PADDED - SHARD))).reshape(-1, 32 * PADDED)


def drop_padding(v):
    return v.reshape(-1, 32, PADDED)[:, :, :SHARD].reshape(-1, MODEL)


def band_valid(block_idx):
    query_pos = block_idx * 128 + jnp.arange(128)[:, None]
    key_pos = block_idx * 128 - WINDOW + jnp.arange(WINDOW + 128)[None, :]
    return (key_pos <= query_pos) & (key_pos > query_pos - WINDOW) & (key_pos >= 0)


def attend(query, keys, values, valid):
    scores = dot_nt(query, keys) * 0.125
    weights = jnp.where(valid, jnp.exp(scores), 0.0)
    prob = weights / jnp.sum(weights, axis=-1, keepdims=True)
    prob_bf = bf(prob)
    return bf(dot(prob_bf, values)), prob, prob_bf


def attend_back(query, keys, values, prob, prob_bf, grad_out):
    grad_prob = dot_nt(grad_out, values)
    grad_value = dot_tn(prob_bf, grad_out)
    grad_score = bf(
        prob * (grad_prob - jnp.sum(grad_prob * prob, axis=-1, keepdims=True)) * 0.125
    )
    return dot(grad_score, keys), dot_tn(grad_score, query), grad_value


def heads_first(v):
    return v.reshape(128, GROUP, HEAD_SIZE).transpose(1, 0, 2).reshape(GROUP * 128, HEAD_SIZE)


def heads_last(v):
    return v.reshape(GROUP, 128, HEAD_SIZE).transpose(1, 0, 2).reshape(128, GROUP * HEAD_SIZE)


def pack_rows(main_t, extra_t, rows):
    low = dot(main_t, rows[:, :HALF_LANES])
    high = dot(main_t, rows[:, HALF_LANES:])
    padded = jnp.pad(rows, ((0, 0), (0, 192)))
    quarters = jnp.concatenate([padded[:, 768 * q : 768 * q + 768] for q in range(4)], axis=0)
    extra = dot(extra_t, quarters)
    return low, high, extra


def join(low, high, extra):
    second = jnp.concatenate(
        [bf(high), jnp.zeros((512, 64), jnp.bfloat16), bf(extra), jnp.zeros((512, 128), jnp.bfloat16)],
        axis=1,
    )
    return jnp.stack([bf(low), second]).reshape(2, 32, 16, HALF_LANES)


def unpack_rows(packed):
    packed = packed.reshape(2, 512, HALF_LANES)
    main = jnp.concatenate([packed[0], packed[1, :, :960]], axis=1)
    extra = packed[1, :, 1024:1792].reshape(32, 4, 4, 768).transpose(0, 2, 1, 3).reshape(128, 3072)
    return jnp.concatenate([main, extra[:, :MODEL]], axis=0)


def repack_rows(rows):
    main, extra = rows[:512], jnp.pad(rows[512:], ((0, 0), (0, 192)))
    extra = extra.reshape(32, 4, 4, 768).transpose(0, 2, 1, 3).reshape(512, 768)
    zeros = lambda n: jnp.zeros((512, n), jnp.bfloat16)
    second = jnp.concatenate([main[:, HALF_LANES:], zeros(64), extra, zeros(128)], axis=1)
    return jnp.stack([main[:, :HALF_LANES], second]).reshape(2, 32, 16, HALF_LANES)


def combine(main_w, extra_w, back, core):
    back = back.reshape(512, HALF_LANES)
    main = dot(main_w, back)
    extra = [dot(extra_w[:, 512 * q : 512 * q + 512], back[:, 1024:1792]) for q in range(4)]
    extra = jnp.concatenate(extra, axis=1)[:, :MODEL]
    first = jnp.pad(main, ((0, 0), (0, MODEL - HALF_LANES)))
    second = jnp.pad(main[:, :960], ((0, 0), (HALF_LANES, 0))) + extra
    return jnp.where(core == 0, first, second)


def add_base(total, mine, base):
    return bf(f32(base[mine, :]) + total)


def finish_resid(total, mine, cot, resid, grad_resid):
    values = f32(resid[mine, :])
    out = f32(cot[mine, :]) + rms_back(values, inverse_rms(values), total)
    grad_resid[...] = out
    return bf(out)


def finish_tokens(total, mine, tokens, grad_resid):
    values = f32(tokens[mine, :])
    return bf(grad_resid[...] + rms_back(values, inverse_rms(values), total))


def body(
    tokens, cotangent, expert_ids, combine_weights,
    w_query, key_value_weight, w_output, w_gate, w_up, w_down,
):
    ctx_block = lax.axis_index(CTX)
    core = lax.axis_index(EXP) % 2
    tokens_f32 = f32(tokens)
    normed = bf(tokens_f32 * inverse_rms(tokens_f32))
    normed_pad = pad_features(normed)
    shard = jnp.concatenate([w_query, key_value_weight, w_output.T], axis=1)
    full = gather_weights(jnp.pad(shard, ((0, PADDED - SHARD), (0, 0))))

    named = expert_ids[:, :, None] == jnp.arange(32)[None, None, :]
    hot = jnp.any(named, axis=1)
    weight = jnp.sum(jnp.where(named, combine_weights[:, :, None], 0.0), axis=1)
    order = jnp.arange(128)
    earlier = dot(bf(order[:, None] > order[None, :]), bf(hot))
    slots = jnp.arange(512)
    widen = bf(jnp.arange(32)[:, None] == slots[None, :] // 16)
    slot_of = dot(bf(jnp.where(hot, earlier, 64.0)), widen)
    weight_of = jnp.repeat(weight, 16, axis=1)
    is_main = slot_of == f32(slots % 16)[None, :]
    is_extra = slot_of == f32(16 + slots % 4)[None, :]
    quarter = [is_extra & (slots % 16 // 4 == q)[None, :] for q in range(4)]
    main_t = bf(is_main).T
    extra_t = jnp.concatenate([bf(q) for q in quarter], axis=0).T
    main_scale = jnp.sum(jnp.where(is_main, weight_of, 0.0), axis=0)[:, None]
    extra_scale = jnp.sum(jnp.where(is_extra, weight_of, 0.0), axis=0)[:, None]

    low, high, extra = pack_rows(main_t, extra_t, cotangent)
    grad_packed = join(low * main_scale, high * main_scale, extra * extra_scale)

    projected = bf(dot(normed_pad, full[:, :384]))
    query_matrix, key_value = projected[:, :256], projected[:, 256:]
    prev_rim = shifted(key_value, 1)
    span = jnp.concatenate([prev_rim, key_value], axis=0)
    keys, values = span[:, :HEAD_SIZE], span[:, HEAD_SIZE:]
    valid = jnp.tile(band_valid(ctx_block), (GROUP, 1))
    query = heads_first(query_matrix)
    attended, prob, prob_bf = attend(query, keys, values, valid)
    attended = heads_last(attended)
    head_part = bf(drop_padding(dot_nt(attended, full[:, 384:])))
    (residual,) = sum_heads(head_part, add_base, [tokens], 4, name="residual")
    residual_f32 = f32(residual)
    moe_input = bf(residual_f32 * inverse_rms(residual_f32))
    row_packed = join(*pack_rows(main_t, extra_t, moe_input))
    rows, grads = dispatch(row_packed, grad_packed)
    expert_rows, grad_expert = unpack_rows(rows), unpack_rows(grads)

    gate_pre = dot(expert_rows, w_gate[0])
    up_pre = dot(expert_rows, w_up[0])
    gate_sig = jax.nn.sigmoid(GLU_ALPHA * gate_pre)
    gate_glu = gate_pre * gate_sig
    activated = bf(gate_glu * (up_pre + 1.0))
    down_part = bf(dot(activated, w_down[0]))
    grad_act = dot_nt(grad_expert, w_down[0])
    grad_gate_pre = bf(
        grad_act * (up_pre + 1.0) * (gate_sig + GLU_ALPHA * gate_glu * (1.0 - gate_sig))
    )
    grad_up_pre = bf(grad_act * gate_glu)
    grad_down = bf(dot_tn(activated, grad_expert))[None]
    grad_gate = bf(dot_tn(expert_rows, grad_gate_pre))[None]
    grad_up = bf(dot_tn(expert_rows, grad_up_pre))[None]
    input_part = bf(dot_nt(grad_gate_pre, w_gate[0]) + dot_nt(grad_up_pre, w_up[0]))
    input_back, down_back = giveback(repack_rows(input_part), repack_rows(down_part))

    extra_w = extra_t.T
    extra_one = jnp.concatenate([bf(q) for q in quarter], axis=1)
    grad_normed = combine(bf(is_main), extra_one, input_back, core)
    weighted = lambda m: jnp.where(m, weight_of, 0.0)
    whole_w = jnp.concatenate([weighted(is_main)] + [weighted(q) for q in quarter], axis=1)
    high_w = bf(whole_w)
    low_w = bf(whole_w - f32(high_w))
    moe_part = combine(high_w[:, :512], high_w[:, 512:], down_back, core) + combine(
        low_w[:, :512], low_w[:, 512:], down_back, core
    )
    own = jax.ShapeDtypeStruct((16, MODEL), jnp.float32)
    grad_resid_bf, grad_resid = sum_heads(
        bf(grad_normed), finish_resid, [cotangent, residual], 5, (own,), name="grad_residual"
    )
    (block_out,) = sum_heads(bf(moe_part), add_base, [residual], 4, name="block_out")
    resid_pad = pad_features(grad_resid_bf)
    attended_grad = bf(dot(resid_pad, full[:, 384:]))
    query_grads, key_grads, value_grads = attend_back(
        query, keys, values, prob, prob_bf, heads_first(attended_grad)
    )
    span_grads = jnp.concatenate([key_grads, value_grads], axis=1)
    rim_grad = f32(shifted(bf(span_grads[:WINDOW]), -1))
    key_value_grad = bf(span_grads[WINDOW:] + rim_grad)
    query_grad = heads_last(bf(query_grads))
    qkv_grad = jnp.concatenate([query_grad, key_value_grad], axis=1)
    grad_part = bf(drop_padding(dot_nt(qkv_grad, full[:, :384])))
    (grad_tokens,) = sum_heads(grad_part, finish_tokens, [tokens, grad_resid], 6, name="grad_tokens")
    terms = bf(jnp.concatenate([dot_tn(normed_pad, qkv_grad), dot_tn(resid_pad, attended)], axis=1))
    sums = scatter_sums(terms)[:SHARD]
    return (
        block_out, grad_tokens, sums[:, :256], sums[:, 256:384], sums[:, 384:].T,
        grad_gate, grad_up, grad_down,
    )


def solution(mesh):
    in_specs = (
        P("ctx", None), P("ctx", None), P("ctx", None), P("ctx", None),
        P("ctx", "exp"), P("ctx", "exp"), P("exp", "ctx"),
        P("ctx", None, "exp"), P("ctx", None, "exp"), P("ctx", "exp", None),
    )
    out_specs = (
        P("ctx", None), P("ctx", None), P("ctx", "exp"), P("ctx", "exp"), P("exp", "ctx"),
        P("ctx", None, "exp"), P("ctx", None, "exp"), P("ctx", "exp", None),
    )
    return jax.shard_map(body, mesh=mesh, in_specs=in_specs, out_specs=out_specs, check_vma=False)
```

time: 900 us -> 538 us (0.60)
  the two profiles are of different devices: /device:TPU:82 before, /device:TPU:1 now
where the time goes in v1:
time: 538 us; the launch traced here: 530 us
  Pallas kernels  333 us (62%)
  local copies, waits for them, and re-layouts  87.4 us (16%)
  matrix products  63.4 us (12%)
  other arithmetic  38.3 us (7%)
    pallas_call x4, Pallas kernels, sum_heads(): pl.pallas_call(functools.partial(sum_kernel, post, len(ins), len(extra_ou...  125 us
    pallas_call x1, Pallas kernels, dispatch(): pl.pallas_call(functools.partial(dispatch_kernel, count), out_shape=[shap...  72.7 us
    pallas_call x1, Pallas kernels, giveback(): pl.pallas_call(functools.partial(giveback_kernel, count), out_shape=[jax....  69.7 us
    dot_general x29, matrix products, dot(): return jnp.dot(a, b, preferred_element_type=jnp.float32)  36.1 us
    pallas_call x1, Pallas kernels, gather_weights(): pl.pallas_call(gather_kernel, out_shape=jax.ShapeDtypeStruct((2, 4, 4, PA...  33.8 us
    pallas_call x1, Pallas kernels, scatter_sums(): pl.pallas_call(scatter_kernel, out_shape=jax.ShapeDtypeStruct((PADDED, 64...  32.6 us
    unnamed x148, local copies, waits for them, and re-layouts  15.8 us
    dot_general x7, matrix products, dot_tn(): lax.dot_general(a, b, (((0,), (0,)), ((), ())), preferred_element_type=jn...  14.9 us
  transfers between devices with their start and end apart: 2, of which 0 were waited for; matrix products, arithmetic and copies ran while one was open for 5% of the time, Pallas kernels for 6%

profile of v1, /device:TPU:1, one launch (start us, length us, event | category | flops | bytes accessed | tf_op | source)
XLA Modules:
  0.0 529.5 jit_solution(10384362219828883553)
XLA Ops:
  2.3 33.8 %gather_weights.1 = bf16[2,4,4,96,640]{4,3,2,1,0:T(8,128)(2,1)} custom-call(bf16[96,640]{1,0:T(8,128)(2,1)} %fusion.104.w_ref), custom_call_target="tpu_custom_call" | custom-call | tf_op jit(solution)/shard_map/gather_weights/pallas_call | solution.py:109
  42.2 3.5 collective-permute-start
  62.1 2.7 slice.277
  74.7 35.8 %residual.1.refs_1_.refs_2_ = bf16[128,2880]{1,0:T(8,128)(2,1)} custom-call(bf16[128,2880]{1,0:T(8,128)(2,1)} %copy.92.refs_0_, bf16[128,2880]{1,0:T(8,128)(2,1)} %copy.93.refs_1_), custom_call_target="tpu_custom_call" | custom-call | tf_op jit(solution)/shard_map/residual/pallas_call | solution.py:437
  117.2 4.0 maximum_maximum_fusion.1
  121.2 4.0 copy.98
  127.6 4.6 pad_maximum_fusion.1.refs_1_
  134.5 72.7 %dispatch_rows.1 = (bf16[2,32,16,1920]{3,2,1,0:T(8,128)(2,1)}, bf16[2,32,16,1920]{3,2,1,0:T(8,128)(2,1)}) custom-call(bf16[2,32,16,1920]{3,2,1,0:T(8,128)(2,1)} %pad_maximum_fusion.refs_0_, bf16[2,32,16,1920]{3,2,1,0:T(8,128)(2,1)} %pad_maximum_fusion.1.refs_1_), custom_call_target="tpu_custom_call" | custom-call | tf_op jit(solution)/shard_map/dispatch_rows/pallas_call | solution.py:304
  207.3 3.1 slice.234
  222.5 3.2 fusion.6
  227.0 4.0 multiply_convert_fusion.3
  230.9 4.6 fusion.2
  243.5 2.5 fusion.1
  255.0 2.9 concatenate.102
  274.3 4.0 concatenate.103
  278.3 3.9 pad_maximum_fusion.3.refs_1_
  282.2 4.0 concatenate.100
  286.2 3.8 pad_maximum_fusion.2.refs_0_
  290.0 69.7 %return_rows.1 = (bf16[32,16,1920]{2,1,0:T(8,128)(2,1)}, bf16[32,16,1920]{2,1,0:T(8,128)(2,1)}) custom-call(bf16[2,32,16,1920]{3,2,1,0:T(8,128)(2,1)} %pad_maximum_fusion.2.refs_0_, bf16[2,32,16,1920]{3,2,1,0:T(8,128)(2,1)} %pad_maximum_fusion.3.refs_1_), custom_call_target="tpu_custom_call" | custom-call | tf_op jit(solution)/shard_map/return_rows/pallas_call | solution.py:363
  376.1 28.8 %grad_residual.1 = (bf16[128,2880]{1,0:T(8,128)(2,1)}, f32[16,2880]{1,0:T(8,128)}) custom-call(bf16[128,2880]{1,0:T(8,128)(2,1)} %fusion.11.refs_0_, bf16[128,2880]{1,0:T(8,128)(2,1)} %copy.109.refs_1_, bf16[128,2880]{1,0:T(8,128)(2,1)} %residual.1.refs_1_.refs_2_), custom_call_target="tpu_custom_call" | custom-call | tf_op jit(solution)/shard_map/grad_residual/pallas_call | solution.py:437
  420.5 31.4 %block_out.1 = bf16[128,2880]{1,0:T(8,128)(2,1)} custom-call(bf16[128,2880]{1,0:T(8,128)(2,1)} %fusion.15.refs_0_, bf16[128,2880]{1,0:T(8,128)(2,1)} %residual.1.refs_1_.refs_2_), custom_call_target="tpu_custom_call" | custom-call | tf_op jit(solution)/shard_map/block_out/pallas_call | solution.py:437
  458.7 32.6 %scatter_sums.1 = bf16[96,640]{1,0:T(8,128)(2,1)} custom-call(bf16[2,4,4,96,640]{4,3,2,1,0:T(8,128)(2,1)} %pad_maximum_fusion.4.t_ref), custom_call_target="tpu_custom_call" | custom-call | tf_op jit(solution)/shard_map/scatter_sums/pallas_call | solution.py:210
  494.1 2.5 convolution_convert_fusion.4
  498.4 28.6 %grad_tokens.1 = bf16[128,2880]{1,0:T(8,128)(2,1)} custom-call(bf16[128,2880]{1,0:T(8,128)(2,1)} %copy.117.refs_0_, bf16[128,2880]{1,0:T(8,128)(2,1)} %copy.93.refs_1_, f32[16,2880]{1,0:T(8,128)} %get-tuple-element.19.refs_2_), custom_call_target="tpu_custom_call" | custom-call | tf_op jit(solution)/shard_map/grad_tokens/pallas_call | solution.py:437
  (287 shorter events, 136.8 us)
Async XLA Ops:
  0.6 226.3 %copy-start = (bf16[1,2880,256]{2,1,0:T(8,128)(2,1)S(1)}, bf16[1,2880,256]{2,1,0:T(8,128)(2,1)}, u32[]{:S(2)}) copy-start(bf16[1,2880,256]{2,1,0:T(8,128)(2,1)} %param.18) | copy-start | bytes 4423684
  2.3 33.8 %copy-start.11 = (bf16[128,2880]{0,1:T(8,128)(2,1)S(1)}, bf16[128,2880]{0,1:T(8,128)(2,1)}, u32[]{:S(2)}) copy-start(bf16[128,2880]{0,1:T(8,128)(2,1)} %param.10) | copy-start | bytes 2211844
  38.9 10.5 %copy-start.60 = (s32[128,4]{0,1:T(4,128)S(1)}, s32[128,4]{0,1:T(4,128)}, u32[]{:S(2)}) copy-start(s32[128,4]{0,1:T(4,128)} %param.12) | copy-start | bytes 6148
  38.9 10.5 %copy-start.61 = (f32[128,4]{0,1:T(4,128)S(1)}, f32[128,4]{0,1:T(4,128)}, u32[]{:S(2)}) copy-start(f32[128,4]{0,1:T(4,128)} %param.13) | copy-start | bytes 6148
  39.8 9.8 %copy-start.4 = (bf16[128,2880]{0,1:T(8,128)(2,1)S(1)}, bf16[128,2880]{0,1:T(8,128)(2,1)}, u32[]{:S(2)}) copy-start(bf16[128,2880]{0,1:T(8,128)(2,1)} %param.11) | copy-start | bytes 2211844
  42.1 7.3 %copy-start.53 = (bf16[128,384]{1,0:T(8,128)(2,1)}, bf16[128,384]{1,0:T(8,128)(2,1)S(1)}, u32[]{:S(2)}) copy-start(bf16[128,384]{1,0:T(8,128)(2,1)S(1)} %fusion.34) | copy-start | bytes 294916
  42.2 25.3 %collective-permute-start = (bf16[128,128]{1,0:T(8,128)(2,1)S(1)}, bf16[128,128]{1,0:T(8,128)(2,1)}, u32[]{:S(2)}, u32[]{:S(2)}) collective-permute-start(bf16[128,128]{1,0:T(8,128)(2,1)S(1)} %slice.273), channel_id=1, source_target_pairs={{0,8},{8,16},{16,24},{24,32},{32,40},{40,48},{48,56},{56,64},{64,7... | collective-permute-start | bytes 98312 | tf_op jit(solution)/shard_map/ppermute | solution.py:489
  49.7 4.6 copy-start.68
  50.6 4.4 copy-start.66
  53.5 62.3 %copy-start.43 = (pred[128,512]{1,0:T(32,128)(4,1)}, pred[128,512]{1,0:T(32,128)(4,1)S(1)}, u32[]{:S(2)}) copy-start(pred[128,512]{1,0:T(32,128)(4,1)S(1)} %get-tuple-element.55) | copy-start | bytes 196612
  54.2 61.6 %copy-start.45 = (pred[128,512]{1,0:T(32,128)(4,1)}, pred[128,512]{1,0:T(32,128)(4,1)S(1)}, u32[]{:S(2)}) copy-start(pred[128,512]{1,0:T(32,128)(4,1)S(1)} %get-tuple-element.53) | copy-start | bytes 196612
  55.0 5.4 %copy-start.47 = (pred[128,512]{1,0:T(32,128)(4,1)}, pred[128,512]{1,0:T(32,128)(4,1)S(1)}, u32[]{:S(2)}) copy-start(pred[128,512]{1,0:T(32,128)(4,1)S(1)} %get-tuple-element.51) | copy-start | bytes 196612
  55.8 4.6 copy-start.50
  127.6 4.6 copy-start.7
  127.6 4.6 copy-start.10
  207.3 6.6 %copy-start.18 = (bf16[2,32,16,1920]{3,2,1,0:T(8,128)(2,1)S(1)}, bf16[2,32,16,1920]{3,2,1,0:T(8,128)(2,1)}, u32[]{:S(2)}) copy-start(bf16[2,32,16,1920]{3,2,1,0:T(8,128)(2,1)} %get-tuple-element.15) | copy-start | bytes 11796484
  255.0 5.1 copy-start.5
  265.8 4.7 copy-start.6
  274.3 4.0 copy-start.8
  282.2 4.0 copy-start.9
  290.0 69.7 %copy-start.52 = (pred[128,512]{1,0:T(32,128)(4,1)S(1)}, pred[128,512]{1,0:T(32,128)(4,1)}, u32[]{:S(2)}) copy-start(pred[128,512]{1,0:T(32,128)(4,1)} %copy-done.50) | copy-start | bytes 196612
  290.0 71.3 %copy-start.49 = (pred[128,512]{1,0:T(32,128)(4,1)S(1)}, pred[128,512]{1,0:T(32,128)(4,1)}, u32[]{:S(2)}) copy-start(pred[128,512]{1,0:T(32,128)(4,1)} %copy-done.47) | copy-start | bytes 196612
  365.2 50.3 %copy-start.12 = (f32[128,1920]{1,0:T(8,128)}, f32[128,1920]{1,0:T(8,128)S(1)}, u32[]{:S(2)}) copy-start(f32[128,1920]{1,0:T(8,128)S(1)} %fusion.97) | copy-start | bytes 2949124
  413.9 40.2 %collective-permute-start.1 = (bf16[128,128]{0,1:T(8,128)(2,1)S(1)}, bf16[128,128]{0,1:T(8,128)(2,1)S(1)}, u32[]{:S(2)}, u32[]{:S(2)}) collective-permute-start(bf16[128,128]{0,1:T(8,128)(2,1)S(1)} %fusion.115), channel_id=1, source_target_pairs={{8,0},{16,8},{24,16},{32,24},{40,32},{48,40},{56,48},{64,56},{72,6... | collective-permute-start | bytes 98312 | tf_op jit(solution)/shard_map/ppermute | solution.py:489
  (52 other events, 129.7 us)

commit v2 on v1

--- a/solution.py
+++ b/solution.py
@@ -230,150 +230,6 @@
     )(terms.reshape(2, 4, 4, PADDED, 640))
 
 
-def shifted_by(z, y, x, i, sign):
-    dz, dy, dx = i // 16, (i // 4) % 4, i % 4
-    return ((z + dz) % 2) * 16 + ((y + sign * dy + 4) % 4) * 4 + (x + sign * dx + 4) % 4
-
-
-def greet_all(c, z, y, x, e, partner):
-    barrier = pltpu.get_barrier_semaphore()
-
-    def hello(i, carry):
-        pl.semaphore_signal(
-            barrier, inc=1, device_id=(shifted_by(z, y, x, i, 1), e), device_id_type=MESH
-        )
-        return carry
-
-    lax.fori_loop(1, 32, hello, 0)
-    pl.semaphore_signal(barrier, inc=1, device_id=partner, device_id_type=MESH)
-    pl.semaphore_wait(barrier, 32)
-
-
-def dispatch_kernel(arrays, *refs):
-    ins, outs = refs[:arrays], refs[arrays : 2 * arrays]
-    send, recv, send2, recv2 = refs[2 * arrays :]
-    c, z, y, x = place()
-    e = lax.axis_index(EXP)
-    k = e % 2
-    partner = (c, e + 1 - 2 * k)
-    greet_all(c, z, y, x, e, partner)
-    for a in range(arrays):
-        outs[a][k, c] = ins[a][k, c]
-
-    def out_copy(a, i):
-        to = shifted_by(z, y, x, i, 1)
-        return pltpu.make_async_remote_copy(
-            src_ref=ins[a].at[k, to], dst_ref=outs[a].at[k, c],
-            send_sem=send.at[a, i], recv_sem=recv.at[a, i],
-            device_id=(to, e), device_id_type=MESH,
-        )
-
-    def across(a, i):
-        source = shifted_by(z, y, x, i, -1)
-        return pltpu.make_async_remote_copy(
-            src_ref=outs[a].at[k, source], dst_ref=outs[a].at[k, source],
-            send_sem=send2.at[a, i], recv_sem=recv2.at[a, i],
-            device_id=partner, device_id_type=MESH,
-        )
-
-    for a in range(arrays):
-        lax.fori_loop(1, 32, lambda i, t, a=a: (out_copy(a, i).start(), t)[1], 0)
-    for a in range(arrays):
-        across(a, 0).start()
-
-    def arrived(a, i, t):
-        out_copy(a, i).wait_recv()
-        across(a, i).start()
-        return t
-
-    for a in range(arrays):
-        lax.fori_loop(1, 32, lambda i, t, a=a: arrived(a, i, t), 0)
-
-    def ended(a, i, t):
-        across(a, i).wait()
-        return t
-
-    for a in range(arrays):
-        lax.fori_loop(0, 32, lambda i, t, a=a: ended(a, i, t), 0)
-        lax.fori_loop(1, 32, lambda i, t, a=a: (out_copy(a, i).wait_send(), t)[1], 0)
-
-
-def dispatch(*packed):
-    count = len(packed)
-    shape = jax.ShapeDtypeStruct((2, 32, 16, HALF_LANES), jnp.bfloat16)
-    return pl.pallas_call(
-        functools.partial(dispatch_kernel, count),
-        out_shape=[shape] * count,
-        in_specs=vmem_specs(count),
-        out_specs=vmem_specs(count),
-        scratch_shapes=[pltpu.SemaphoreType.DMA((count, 32))] * 4,
-        compiler_params=params(2),
-        name="dispatch_rows",
-    )(*packed)
-
-
-def giveback_kernel(arrays, *refs):
-    ins, outs = refs[:arrays], refs[arrays : 2 * arrays]
-    other, stage, send, recv, send2, recv2 = refs[2 * arrays :]
-    c, z, y, x = place()
-    e = lax.axis_index(EXP)
-    k = e % 2
-    partner = (c, e + 1 - 2 * k)
-    greet_all(c, z, y, x, e, partner)
-
-    def across(a, i):
-        to = shifted_by(z, y, x, i, 1)
-        return pltpu.make_async_remote_copy(
-            src_ref=ins[a].at[1 - k, to], dst_ref=other.at[a, to],
-            send_sem=send2.at[a, i], recv_sem=recv2.at[a, i],
-            device_id=partner, device_id_type=MESH,
-        )
-
-    def home(a, i):
-        to = shifted_by(z, y, x, i, 1)
-        return pltpu.make_async_remote_copy(
-            src_ref=stage.at[a, to], dst_ref=outs[a].at[c],
-            send_sem=send.at[a, i], recv_sem=recv.at[a, i],
-            device_id=(to, e), device_id_type=MESH,
-        )
-
-    for a in range(arrays):
-        lax.fori_loop(1, 32, lambda i, t, a=a: (across(a, i).start(), t)[1], 0)
-        across(a, 0).start()
-
-    def added(a, i, t):
-        across(a, i).wait_recv()
-        to = shifted_by(z, y, x, i, 1)
-        stage[a, to] = bf(f32(ins[a][k, to]) + f32(other[a, to]))
-        home(a, i).start()
-        return t
-
-    for a in range(arrays):
-        lax.fori_loop(1, 32, lambda i, t, a=a: added(a, i, t), 0)
-        across(a, 0).wait_recv()
-        outs[a][c] = bf(f32(ins[a][k, c]) + f32(other[a, c]))
-    for a in range(arrays):
-        lax.fori_loop(1, 32, lambda i, t, a=a: (home(a, i).wait(), t)[1], 0)
-        lax.fori_loop(0, 32, lambda i, t, a=a: (across(a, i).wait_send(), t)[1], 0)
-
-
-def giveback(*parts):
-    count = len(parts)
-    b = jnp.bfloat16
-    return pl.pallas_call(
-        functools.partial(giveback_kernel, count),
-        out_shape=[jax.ShapeDtypeStruct((32, 16, HALF_LANES), b)] * count,
-        in_specs=vmem_specs(count),
-        out_specs=vmem_specs(count),
-        scratch_shapes=[
-            pltpu.VMEM((count, 32, 16, HALF_LANES), b),
-            pltpu.VMEM((count, 32, 16, HALF_LANES), b),
-        ] + [pltpu.SemaphoreType.DMA((count, 32))] * 4,
-        compiler_params=params(3),
-        name="return_rows",
-    )(*parts)
-
-
 def sum_kernel(post, extra_in, extra_out, *refs):
     part = refs[0]
     ins = refs[1 : 1 + extra_in]
@@ -528,46 +384,309 @@
     return v.reshape(GROUP, 128, HEAD_SIZE).transpose(1, 0, 2).reshape(128, GROUP * HEAD_SIZE)
 
 
-def pack_rows(main_t, extra_t, rows):
-    low = dot(main_t, rows[:, :HALF_LANES])
-    high = dot(main_t, rows[:, HALF_LANES:])
-    padded = jnp.pad(rows, ((0, 0), (0, 192)))
-    quarters = jnp.concatenate([padded[:, 768 * q : 768 * q + 768] for q in range(4)], axis=0)
-    extra = dot(extra_t, quarters)
-    return low, high, extra
-
-
-def join(low, high, extra):
-    second = jnp.concatenate(
-        [bf(high), jnp.zeros((512, 64), jnp.bfloat16), bf(extra), jnp.zeros((512, 128), jnp.bfloat16)],
-        axis=1,
-    )
-    return jnp.stack([bf(low), second]).reshape(2, 32, 16, HALF_LANES)
-
-
-def unpack_rows(packed):
-    packed = packed.reshape(2, 512, HALF_LANES)
-    main = jnp.concatenate([packed[0], packed[1, :, :960]], axis=1)
-    extra = packed[1, :, 1024:1792].reshape(32, 4, 4, 768).transpose(0, 2, 1, 3).reshape(128, 3072)
-    return jnp.concatenate([main, extra[:, :MODEL]], axis=0)
-
-
-def repack_rows(rows):
-    main, extra = rows[:512], jnp.pad(rows[512:], ((0, 0), (0, 192)))
-    extra = extra.reshape(32, 4, 4, 768).transpose(0, 2, 1, 3).reshape(512, 768)
-    zeros = lambda n: jnp.zeros((512, n), jnp.bfloat16)
-    second = jnp.concatenate([main[:, HALF_LANES:], zeros(64), extra, zeros(128)], axis=1)
-    return jnp.stack([main[:, :HALF_LANES], second]).reshape(2, 32, 16, HALF_LANES)
-
-
-def combine(main_w, extra_w, back, core):
-    back = back.reshape(512, HALF_LANES)
-    main = dot(main_w, back)
-    extra = [dot(extra_w[:, 512 * q : 512 * q + 512], back[:, 1024:1792]) for q in range(4)]
-    extra = jnp.concatenate(extra, axis=1)[:, :MODEL]
-    first = jnp.pad(main, ((0, 0), (0, MODEL - HALF_LANES)))
-    second = jnp.pad(main[:, :960], ((0, 0), (HALF_LANES, 0))) + extra
-    return jnp.where(core == 0, first, second)
+def iota(shape, axis):
+    return lax.broadcasted_iota(jnp.int32, shape, axis)
+
+
+def spread_extra(q):
+    r, j = iota((128, 512), 0), iota((128, 512), 1)
+    return bf((j == (r // 4) * 16 + q * 4 + r % 4).astype(jnp.float32))
+
+
+def expert_kernel(
+    x_ref, cot_ref, ids_ref, combine_ref, wg, wu, wd,
+    grad_in_part, moe_part, grad_gate, grad_up, grad_down,
+    xp, one_hot, extra_hot, weight_ref, scale, send_buf, got, ext, gate_pre, up_pre, act, gg, gu, parts, other, back,
+    send, recv, send2, recv2, send3, recv3, send4, recv4,
+):
+    c = lax.axis_index(CTX)
+    e = lax.axis_index(EXP)
+    k = e % 2
+    partner = (c, e + 1 - 2 * k)
+    group, inner = c // 8, c % 8
+    barrier = pltpu.get_barrier_semaphore()
+
+    def moved(n, sign):
+        return ((group + sign * (n // 8) + 4) % 4) * 8 + (inner + sign * (n % 8) + 8) % 8
+
+    def hello(n, t):
+        pl.semaphore_signal(barrier, inc=1, device_id=(moved(n, 1), e), device_id_type=MESH)
+        return t
+
+    lax.fori_loop(1, 32, hello, 0)
+    pl.semaphore_signal(barrier, inc=1, device_id=partner, device_id_type=MESH)
+
+    lane = iota((128, 512), 1)
+    hot = jnp.zeros((128, 512), jnp.float32)
+    weight = jnp.zeros((128, 512), jnp.float32)
+    for route in range(4):
+        match = ids_ref[:, route : route + 1] == lane // 16
+        hot = jnp.where(match, 1.0, hot)
+        weight = jnp.where(match, combine_ref[:, route : route + 1], weight)
+    weight_ref[...] = weight
+    below = bf(jnp.where(iota((128, 128), 0) > iota((128, 128), 1), 1.0, 0.0))
+    slot = jnp.where(hot > 0, dot(below, bf(hot)), 64.0)
+    main = slot == f32(lane % 16)
+    extra = slot == f32(16 + lane % 4)
+    one_hot[...] = bf(jnp.where(main, 1.0, 0.0))
+    for q in range(4):
+        extra_hot[q] = bf(jnp.where(extra & (lane % 16 // 4 == q), 1.0, 0.0))
+    scale[0] = jnp.sum(jnp.where(main, weight, 0.0).T, axis=1, keepdims=True)
+    scale[1] = jnp.sum(jnp.where(extra, weight, 0.0).T, axis=1, keepdims=True)
+    for a, ref in enumerate((x_ref, cot_ref)):
+        xp[a, :, :MODEL] = ref[...]
+        xp[a, :, MODEL:] = jnp.zeros((128, 192), jnp.bfloat16)
+
+    def out_copy(a, n):
+        to = moved(n, 1)
+        return pltpu.make_async_remote_copy(
+            src_ref=send_buf.at[a, to], dst_ref=got.at[a, k, c],
+            send_sem=send.at[a, n], recv_sem=recv.at[a, n],
+            device_id=(to, e), device_id_type=MESH,
+        )
+
+    def over(a, n):
+        source = moved(n, -1)
+        return pltpu.make_async_remote_copy(
+            src_ref=got.at[a, k, source], dst_ref=got.at[a, k, source],
+            send_sem=send2.at[a, n], recv_sem=recv2.at[a, n],
+            device_id=partner, device_id_type=MESH,
+        )
+
+    def pack(a, j, t):
+        g = (group + j) % 4
+        at = pl.ds(pl.multiple_of(g * 128, 128), 128)
+        dest = pl.ds(g * 8, 8)
+        m = one_hot[:, at]
+        s0 = scale[0, at, :] if a else 1.0
+        s1 = scale[1, at, :] if a else 1.0
+
+        @pl.when(k == 0)
+        def _():
+            low = dot_tn(m, xp[a, :, :HALF_LANES])
+            send_buf[a, dest] = bf(low * s0 if a else low).reshape(8, 16, HALF_LANES)
+
+        @pl.when(k == 1)
+        def _():
+            high = dot_tn(m, xp[a, :, HALF_LANES:2944])
+            send_buf[a, dest, :, 0:1024] = bf(high * s0 if a else high).reshape(8, 16, 1024)
+            quarters = dot_tn(extra_hot[0, :, at], xp[a, :, 0:768])
+            for q in range(1, 4):
+                quarters = quarters + dot_tn(extra_hot[q, :, at], xp[a, :, 768 * q : 768 * q + 768])
+            send_buf[a, dest, :, 1024:1792] = bf(quarters * s1 if a else quarters).reshape(8, 16, 768)
+            send_buf[a, dest, :, 1792:] = jnp.zeros((8, 16, 128), jnp.bfloat16)
+
+        return t
+
+    def start_group(a, j):
+        first = 1 if j == 0 else 0
+        lax.fori_loop(first, 8, lambda i, t: (out_copy(a, j * 8 + i).start(), t)[1], 0)
+
+    for a in range(2):
+        for j in range(4):
+            pack(a, j, 0)
+            if a == 0 and j == 0:
+                pl.semaphore_wait(barrier, 32)
+            start_group(a, j)
+        got[a, k, c] = send_buf[a, c]
+        over(a, 0).start()
+
+    def arrived(a, n, t):
+        out_copy(a, n).wait_recv()
+        over(a, n).start()
+        return t
+
+    def take(a):
+        lax.fori_loop(1, 32, lambda n, t: arrived(a, n, t), 0)
+        lax.fori_loop(0, 32, lambda n, t: (over(a, n).wait(), t)[1], 0)
+        packed = got[a, 1, :, :, 1024:1792].reshape(512, 768)
+        for q in range(4):
+            ext[a, :, 768 * q : 768 * q + 768] = bf(dot(spread_extra(q), packed))
+
+    def rows_of(a, t):
+        first = got[a, 0, pl.ds(t * 16, 16)].reshape(256, HALF_LANES)
+        second = got[a, 1, pl.ds(t * 16, 16), :, 0:960].reshape(256, 960)
+        return first, second
+
+    def at_rows(t):
+        return pl.ds(pl.multiple_of(t * 256, 256), 256)
+
+    take(0)
+
+    def forward(t, carry):
+        first, second = rows_of(0, t)
+        for w, into in ((wg, gate_pre), (wu, up_pre)):
+            into[at_rows(t), :] = dot(first, w[:HALF_LANES]) + dot(second, w[HALF_LANES:])
+        return carry
+
+    lax.fori_loop(0, 2, forward, 0)
+    for w, into in ((wg, gate_pre), (wu, up_pre)):
+        into[512:, :] = dot(ext[0, :, :MODEL], w[...])
+
+    take(1)
+
+    def pointwise(rows, grad_act):
+        gate, up = gate_pre[rows, :], up_pre[rows, :] + 1.0
+        sig = jax.nn.sigmoid(GLU_ALPHA * gate)
+        glu = gate * sig
+        act[rows, :] = bf(glu * up)
+        gg[rows, :] = bf(grad_act * up * (sig + GLU_ALPHA * glu * (1.0 - sig)))
+        gu[rows, :] = bf(grad_act * glu)
+
+    def backward(t, carry):
+        first, second = rows_of(1, t)
+        pointwise(at_rows(t), dot_nt(first, wd[:, :HALF_LANES]) + dot_nt(second, wd[:, HALF_LANES:]))
+        return carry
+
+    lax.fori_loop(0, 2, backward, 0)
+    pointwise(pl.ds(512, 128), dot_nt(ext[1, :, :MODEL], wd[...]))
+
+    for a in range(2):
+        lax.fori_loop(1, 32, lambda n, t, a=a: (out_copy(a, n).wait_send(), t)[1], 0)
+
+    def across(a, j):
+        block = pl.ds(((group + j) % 4) * 8, 8)
+        return pltpu.make_async_remote_copy(
+            src_ref=parts.at[a, 1 - k, block], dst_ref=other.at[a, block],
+            send_sem=send3.at[a, j], recv_sem=recv3.at[a, j],
+            device_id=partner, device_id_type=MESH,
+        )
+
+    def home(a, n):
+        to = moved(n, 1)
+        return pltpu.make_async_remote_copy(
+            src_ref=send_buf.at[a, to], dst_ref=back.at[a, c],
+            send_sem=send4.at[a, n], recv_sem=recv4.at[a, n],
+            device_id=(to, e), device_id_type=MESH,
+        )
+
+    def result(a, rows):
+        if a == 0:
+            return bf(dot_nt(gg[rows, :], wg[...]) + dot_nt(gu[rows, :], wu[...]))
+        return bf(dot(act[rows, :], wd[...]))
+
+    def add_pair(a, j):
+        across(a, j).wait_recv()
+
+        def one(i, t):
+            n = j * 8 + i
+            to = moved(n, 1)
+            send_buf[a, to] = bf(f32(parts[a, k, to]) + f32(other[a, to]))
+
+            @pl.when(n > 0)
+            def _():
+                home(a, n).start()
+
+            return t
+
+        lax.fori_loop(0, 8, one, 0)
+        if j == 0:
+            back[a, c] = send_buf[a, c]
+
+    steps = [(a, j) for a in range(2) for j in range(4)]
+    for index, (a, j) in enumerate(steps):
+        if j == 0:
+            last = result(a, pl.ds(512, 128))
+            folded = jnp.zeros((512, 768), jnp.float32)
+            for q in range(4):
+                width = 768 if q < 3 else 576
+                piece = dot_tn(spread_extra(q), last[:, 768 * q : 768 * q + width])
+                if q == 3:
+                    piece = jnp.concatenate([piece, jnp.zeros((512, 192), jnp.float32)], axis=1)
+                folded = folded + piece
+            parts[a, 1, :, :, 1024:1792] = bf(folded).reshape(32, 16, 768)
+            parts[a, 1, :, :, 960:1024] = jnp.zeros((32, 16, 64), jnp.bfloat16)
+            parts[a, 1, :, :, 1792:] = jnp.zeros((32, 16, 128), jnp.bfloat16)
+        g = (group + j) % 4
+        rows = result(a, pl.ds(pl.multiple_of(g * 128, 128), 128))
+        parts[a, 0, pl.ds(g * 8, 8)] = rows[:, :HALF_LANES].reshape(8, 16, HALF_LANES)
+        parts[a, 1, pl.ds(g * 8, 8), :, 0:960] = rows[:, HALF_LANES:].reshape(8, 16, 960)
+        across(a, j).start()
+        if index:
+            add_pair(*steps[index - 1])
+    add_pair(*steps[-1])
+
+    def grads_at(columns, lanes, half):
+        x_main = got[0, half, :, :, lanes].reshape(512, lanes.size)
+        g_main = got[1, half, :, :, lanes].reshape(512, lanes.size)
+        x_ext, g_ext = ext[0, :, columns], ext[1, :, columns]
+        grad_gate[columns, :] = bf(dot_tn(x_main, gg[:512, :]) + dot_tn(x_ext, gg[512:, :]))
+        grad_up[columns, :] = bf(dot_tn(x_main, gu[:512, :]) + dot_tn(x_ext, gu[512:, :]))
+        grad_down[:, columns] = bf(dot_tn(act[:512, :], g_main) + dot_tn(act[512:, :], g_ext))
+
+    def lower(i, t):
+        lanes = pl.ds(pl.multiple_of(i * 384, 128), 384)
+        grads_at(lanes, lanes, 0)
+        return t
+
+    lax.fori_loop(0, 5, lower, 0)
+    grads_at(pl.ds(1920, 512), pl.ds(0, 512), 1)
+    grads_at(pl.ds(2432, 448), pl.ds(512, 448), 1)
+
+    for a, into in enumerate((grad_in_part, moe_part)):
+        lax.fori_loop(1, 32, lambda n, t, a=a: (home(a, n).wait_recv(), t)[1], 0)
+
+        def summed(hot, lanes, a=a):
+            rows = back[a, :, :, lanes].reshape(512, lanes.size)
+            if a == 0:
+                return dot(hot, rows)
+            spread = jnp.where(hot > 0, weight_ref[...], 0.0)
+            high = bf(spread)
+            return dot(high, rows) + dot(bf(spread - f32(high)), rows)
+
+        @pl.when(k == 0)
+        def _(into=into, summed=summed):
+            into[:, :HALF_LANES] = bf(summed(one_hot[...], pl.ds(0, HALF_LANES)))
+            into[:, HALF_LANES:] = jnp.zeros((128, 960), jnp.bfloat16)
+
+        @pl.when(k == 1)
+        def _(into=into, summed=summed):
+            upper = summed(one_hot[...], pl.ds(0, 1024))
+            quarters = [summed(extra_hot[q], pl.ds(1024, 768)) for q in range(4)]
+            into[:, 0:768] = bf(quarters[0])
+            into[:, 768:1536] = bf(quarters[1])
+            into[:, 1536:1920] = bf(quarters[2][:, :384])
+            into[:, 1920:2304] = bf(quarters[2][:, 384:] + upper[:, :384])
+            into[:, 2304:] = bf(quarters[3][:, :576] + upper[:, 384:960])
+
+    for a in range(2):
+        lax.fori_loop(1, 32, lambda n, t, a=a: (home(a, n).wait_send(), t)[1], 0)
+        lax.fori_loop(0, 4, lambda j, t, a=a: (across(a, j).wait_send(), t)[1], 0)
+
+
+def experts(moe_input, cotangent, expert_ids, combine_weights, w_gate, w_up, w_down):
+    b = jnp.bfloat16
+    shape = jax.ShapeDtypeStruct
+    return pl.pallas_call(
+        expert_kernel,
+        out_shape=[
+            shape((128, MODEL), b), shape((128, MODEL), b),
+            shape((MODEL, 256), b), shape((MODEL, 256), b), shape((256, MODEL), b),
+        ],
+        in_specs=vmem_specs(7),
+        out_specs=vmem_specs(5),
+        scratch_shapes=[
+            pltpu.VMEM((2, 128, 3072), b),
+            pltpu.VMEM((128, 512), b),
+            pltpu.VMEM((4, 128, 512), b),
+            pltpu.VMEM((128, 512), jnp.float32),
+            pltpu.VMEM((2, 512, 1), jnp.float32),
+            pltpu.VMEM((2, 32, 16, HALF_LANES), b),
+            pltpu.VMEM((2, 2, 32, 16, HALF_LANES), b),
+            pltpu.VMEM((2, 128, 3072), b),
+            pltpu.VMEM((640, 256), jnp.float32),
+            pltpu.VMEM((640, 256), jnp.float32),
+            pltpu.VMEM((640, 256), b),
+            pltpu.VMEM((640, 256), b),
+            pltpu.VMEM((640, 256), b),
+            pltpu.VMEM((2, 2, 32, 16, HALF_LANES), b),
+            pltpu.VMEM((2, 32, 16, HALF_LANES), b),
+            pltpu.VMEM((2, 32, 16, HALF_LANES), b),
+        ] + [pltpu.SemaphoreType.DMA((2, 32))] * 4
+        + [pltpu.SemaphoreType.DMA((2, 4))] * 2 + [pltpu.SemaphoreType.DMA((2, 32))] * 2,
+        compiler_params=params(2),
+        name="experts",
+    )(moe_input, cotangent, expert_ids, combine_weights, w_gate, w_up, w_down)
 
 
 def add_base(total, mine, base):
@@ -591,32 +710,11 @@
     w_query, key_value_weight, w_output, w_gate, w_up, w_down,
 ):
     ctx_block = lax.axis_index(CTX)
-    core = lax.axis_index(EXP) % 2
     tokens_f32 = f32(tokens)
     normed = bf(tokens_f32 * inverse_rms(tokens_f32))
     normed_pad = pad_features(normed)
     shard = jnp.concatenate([w_query, key_value_weight, w_output.T], axis=1)
     full = gather_weights(jnp.pad(shard, ((0, PADDED - SHARD), (0, 0))))
-
-    named = expert_ids[:, :, None] == jnp.arange(32)[None, None, :]
-    hot = jnp.any(named, axis=1)
-    weight = jnp.sum(jnp.where(named, combine_weights[:, :, None], 0.0), axis=1)
-    order = jnp.arange(128)
-    earlier = dot(bf(order[:, None] > order[None, :]), bf(hot))
-    slots = jnp.arange(512)
-    widen = bf(jnp.arange(32)[:, None] == slots[None, :] // 16)
-    slot_of = dot(bf(jnp.where(hot, earlier, 64.0)), widen)
-    weight_of = jnp.repeat(weight, 16, axis=1)
-    is_main = slot_of == f32(slots % 16)[None, :]
-    is_extra = slot_of == f32(16 + slots % 4)[None, :]
-    quarter = [is_extra & (slots % 16 // 4 == q)[None, :] for q in range(4)]
-    main_t = bf(is_main).T
-    extra_t = jnp.concatenate([bf(q) for q in quarter], axis=0).T
-    main_scale = jnp.sum(jnp.where(is_main, weight_of, 0.0), axis=0)[:, None]
-    extra_scale = jnp.sum(jnp.where(is_extra, weight_of, 0.0), axis=0)[:, None]
-
-    low, high, extra = pack_rows(main_t, extra_t, cotangent)
-    grad_packed = join(low * main_scale, high * main_scale, extra * extra_scale)
 
     projected = bf(dot(normed_pad, full[:, :384]))
     query_matrix, key_value = projected[:, :256], projected[:, 256:]
@@ -631,42 +729,14 @@
     (residual,) = sum_heads(head_part, add_base, [tokens], 4, name="residual")
     residual_f32 = f32(residual)
     moe_input = bf(residual_f32 * inverse_rms(residual_f32))
-    row_packed = join(*pack_rows(main_t, extra_t, moe_input))
-    rows, grads = dispatch(row_packed, grad_packed)
-    expert_rows, grad_expert = unpack_rows(rows), unpack_rows(grads)
-
-    gate_pre = dot(expert_rows, w_gate[0])
-    up_pre = dot(expert_rows, w_up[0])
-    gate_sig = jax.nn.sigmoid(GLU_ALPHA * gate_pre)
-    gate_glu = gate_pre * gate_sig
-    activated = bf(gate_glu * (up_pre + 1.0))
-    down_part = bf(dot(activated, w_down[0]))
-    grad_act = dot_nt(grad_expert, w_down[0])
-    grad_gate_pre = bf(
-        grad_act * (up_pre + 1.0) * (gate_sig + GLU_ALPHA * gate_glu * (1.0 - gate_sig))
-    )
-    grad_up_pre = bf(grad_act * gate_glu)
-    grad_down = bf(dot_tn(activated, grad_expert))[None]
-    grad_gate = bf(dot_tn(expert_rows, grad_gate_pre))[None]
-    grad_up = bf(dot_tn(expert_rows, grad_up_pre))[None]
-    input_part = bf(dot_nt(grad_gate_pre, w_gate[0]) + dot_nt(grad_up_pre, w_up[0]))
-    input_back, down_back = giveback(repack_rows(input_part), repack_rows(down_part))
-
-    extra_w = extra_t.T
-    extra_one = jnp.concatenate([bf(q) for q in quarter], axis=1)
-    grad_normed = combine(bf(is_main), extra_one, input_back, core)
-    weighted = lambda m: jnp.where(m, weight_of, 0.0)
-    whole_w = jnp.concatenate([weighted(is_main)] + [weighted(q) for q in quarter], axis=1)
-    high_w = bf(whole_w)
-    low_w = bf(whole_w - f32(high_w))
-    moe_part = combine(high_w[:, :512], high_w[:, 512:], down_back, core) + combine(
-        low_w[:, :512], low_w[:, 512:], down_back, core
+    grad_normed, moe_part, grad_gate, grad_up, grad_down = experts(
+        moe_input, cotangent, expert_ids, combine_weights, w_gate[0], w_up[0], w_down[0]
     )
     own = jax.ShapeDtypeStruct((16, MODEL), jnp.float32)
     grad_resid_bf, grad_resid = sum_heads(
-        bf(grad_normed), finish_resid, [cotangent, residual], 5, (own,), name="grad_residual"
+        grad_normed, finish_resid, [cotangent, residual], 5, (own,), name="grad_residual"
     )
-    (block_out,) = sum_heads(bf(moe_part), add_base, [residual], 4, name="block_out")
+    (block_out,) = sum_heads(moe_part, add_base, [residual], 4, name="block_out")
     resid_pad = pad_features(grad_resid_bf)
     attended_grad = bf(dot(resid_pad, full[:, 384:]))
     query_grads, key_grads, value_grads = attend_back(
@@ -683,7 +753,7 @@
     sums = scatter_sums(terms)[:SHARD]
     return (
         block_out, grad_tokens, sums[:, :256], sums[:, 256:384], sums[:, 384:].T,
-        grad_gate, grad_up, grad_down,
+        grad_gate[None], grad_up[None], grad_down[None],
     )
 
 

time: 538 us -> 388 us (0.72); the launches traced: 530 us -> 387 us
  local copies, waits for them, and re-layouts: 87.4 us -> 27 us
  matrix products: 63.4 us -> 10.2 us
  other arithmetic: 38.3 us -> 9.69 us
    dot_general x29 -> x4, matrix products: 36.1 us -> 4.76 us  [dot(): return jnp.dot(a, b, preferred_element_type=jnp.float32)]
    slice x24 -> x0, local copies, waits for them, and re-layouts: 23.6 us -> none  [the longest x4 7.9 us: repack_rows(): main[:, :HALF_LANES]]
    concatenate x10 -> x0, local copies, waits for them, and re-layouts: 21.1 us -> none  [the longest x6 14.6 us: repack_rows(): jnp.concatenate([main[:, HALF_LANES:], zeros(64), extra, zeros(128)], axi...]
    another operation x5 -> x1, other arithmetic: 14.6 us -> 0.01 us  [the longest x2 7.73 us: repack_rows(): jnp.stack([main[:, :HALF_LANES], second]).reshape(2, 32, 16, HALF_LANES)]
    pallas_call x1, Pallas kernels: 32.6 us -> 46 us  [scatter_sums(): pl.pallas_call(scatter_kernel, out_shape=jax.ShapeDtypeStruct((PADDED, 64...]
    dot_general x7 -> x4, matrix products: 14.9 us -> 1.73 us  [dot_tn(): lax.dot_general(a, b, (((0,), (0,)), ((), ())), preferred_element_type=jn...]
    dot_general x7 -> x4, matrix products: 12.4 us -> 3.65 us  [dot_nt(): lax.dot_general(a, b, (((1,), (1,)), ((), ())), preferred_element_type=jn...]
    pallas_call x4, Pallas kernels: 125 us -> 117 us  [sum_heads(): pl.pallas_call(functools.partial(sum_kernel, post, len(ins), len(extra_ou...]
  transfers between devices with their start and end apart: 2 -> 2, of which waited for: 0 -> 0; matrix products, arithmetic and copies ran while one was open for 5% -> 4% of each run, Pallas kernels for 6% -> 7%
where the time goes in v2:
time: 388 us; the launch traced here: 387 us
  Pallas kernels  335 us (86%)
  local copies, waits for them, and re-layouts  27 us (7%)
  matrix products  10.2 us (3%)
  other arithmetic  9.69 us (2%)
  starting transfers between devices  4.46 us (1%)
    pallas_call x1, Pallas kernels, experts(): pl.pallas_call(expert_kernel, out_shape=[shape((128, MODEL), b), shape((1...  138 us
    pallas_call x4, Pallas kernels, sum_heads(): pl.pallas_call(functools.partial(sum_kernel, post, len(ins), len(extra_ou...  117 us
    pallas_call x1, Pallas kernels, scatter_sums(): pl.pallas_call(scatter_kernel, out_shape=jax.ShapeDtypeStruct((PADDED, 64...  46 us
    pallas_call x1, Pallas kernels, gather_weights(): pl.pallas_call(gather_kernel, out_shape=jax.ShapeDtypeStruct((2, 4, 4, PA...  33.7 us
    unnamed x34, local copies, waits for them, and re-layouts  17 us
  transfers between devices with their start and end apart: 2, of which 0 were waited for; matrix products, arithmetic and copies ran while one was open for 4% of the time, Pallas kernels for 7%

profile of v2, /device:TPU:1, one launch (start us, length us, event | category | flops | bytes accessed | tf_op | source)
XLA Modules:
  0.0 387.3 jit_solution(15401548450842556883)
XLA Ops:
  0.6 1.5 fusion.5
  4.4 33.7 %gather_weights.1 = bf16[2,4,4,96,640]{4,3,2,1,0:T(8,128)(2,1)} custom-call(bf16[96,640]{1,0:T(8,128)(2,1)} %fusion.21.w_ref), custom_call_target="tpu_custom_call" | custom-call | tf_op jit(solution)/shard_map/gather_weights/pallas_call | solution.py:109
  38.2 2.3 fusion.9
  40.5 2.9 collective-permute-start
  44.8 1.6 slice.66
  49.0 2.6 copy.39
  54.9 32.3 %residual.1.refs_1_.refs_2_ = bf16[128,2880]{1,0:T(8,128)(2,1)} custom-call(bf16[128,2880]{1,0:T(8,128)(2,1)} %copy.37.refs_0_, bf16[128,2880]{1,0:T(8,128)(2,1)} %copy.38.refs_1_), custom_call_target="tpu_custom_call" | custom-call | tf_op jit(solution)/shard_map/residual/pallas_call | solution.py:293
  87.1 1.4 fusion.3
  88.5 2.2 fusion.4.x_ref
  90.7 138.1 %experts.1 = (bf16[128,2880]{1,0:T(8,128)(2,1)}, bf16[128,2880]{1,0:T(8,128)(2,1)}, bf16[2880,256]{1,0:T(8,128)(2,1)}, bf16[2880,256]{1,0:T(8,128)(2,1)}, bf16[256,2880]{1,0:T(8,128)(2,1)}) custom-call(bf16[128,2880]{1,0:T(8,128)(2,1)} %fusion.4.x_ref, bf16[128,2880]{1,0:T(8,128)(2,1)} %copy.40.cot_ref.refs_1_, s32[128,4]{1,0:T(8,128)} %copy.41.ids_ref, ...), custom_call_target="tpu_custom_call" | custom-call | tf_op jit(solution)/shard_map/experts/pallas_call | solution.py:660
  228.8 27.5 %grad_residual.1 = (bf16[128,2880]{1,0:T(8,128)(2,1)}, f32[16,2880]{1,0:T(8,128)}) custom-call(bf16[128,2880]{1,0:T(8,128)(2,1)} %get-tuple-element.16.refs_0_, bf16[128,2880]{1,0:T(8,128)(2,1)} %copy.40.cot_ref.refs_1_, bf16[128,2880]{1,0:T(8,128)(2,1)} %residual.1.refs_1_.refs_2_), custom_call_target="tpu_custom_call" | custom-call | tf_op jit(solution)/shard_map/grad_residual/pallas_call | solution.py:293
  256.3 1.5 copy.44
  258.1 1.9 convolution_convert_fusion.3
  261.0 1.6 collective-permute-start.1
  263.4 25.6 %block_out.1 = bf16[128,2880]{1,0:T(8,128)(2,1)} custom-call(bf16[128,2880]{1,0:T(8,128)(2,1)} %get-tuple-element.15.refs_0_, bf16[128,2880]{1,0:T(8,128)(2,1)} %residual.1.refs_1_.refs_2_), custom_call_target="tpu_custom_call" | custom-call | tf_op jit(solution)/shard_map/block_out/pallas_call | solution.py:293
  289.0 2.3 copy.54
  291.4 2.5 copy.56
  294.1 2.5 convolution_convert_fusion
  297.4 2.4 pad_maximum_fusion.t_ref
  299.8 46.0 %scatter_sums.1 = bf16[96,640]{1,0:T(8,128)(2,1)} custom-call(bf16[2,4,4,96,640]{4,3,2,1,0:T(8,128)(2,1)} %pad_maximum_fusion.t_ref), custom_call_target="tpu_custom_call" | custom-call | tf_op jit(solution)/shard_map/scatter_sums/pallas_call | solution.py:210
  345.8 1.3 slice.59
  347.2 1.5 slice_bitcast_fusion
  350.4 31.7 %grad_tokens.1 = bf16[128,2880]{1,0:T(8,128)(2,1)} custom-call(bf16[128,2880]{1,0:T(8,128)(2,1)} %copy.51.refs_0_, bf16[128,2880]{1,0:T(8,128)(2,1)} %copy.38.refs_1_, f32[16,2880]{1,0:T(8,128)} %get-tuple-element.18.refs_2_), custom_call_target="tpu_custom_call" | custom-call | tf_op jit(solution)/shard_map/grad_tokens/pallas_call | solution.py:293
  382.0 2.3 copy.55
  (71 shorter events, 17.1 us)
Async XLA Ops:
  2.1 1.5 copy-start.7
  2.1 1.5 copy-start.8
  2.2 1.5 copy-start.9
  38.2 5.5 %copy-start = (bf16[128,2880]{0,1:T(8,128)(2,1)S(1)}, bf16[128,2880]{0,1:T(8,128)(2,1)}, u32[]{:S(2)}) copy-start(bf16[128,2880]{0,1:T(8,128)(2,1)} %param.10) | copy-start | bytes 2211844
  40.5 5.9 %copy-start.6 = (bf16[128,384]{1,0:T(8,128)(2,1)}, bf16[128,384]{1,0:T(8,128)(2,1)S(1)}, u32[]{:S(2)}) copy-start(bf16[128,384]{1,0:T(8,128)(2,1)S(1)} %fusion.9) | copy-start | bytes 294916
  40.5 11.2 %collective-permute-start = (bf16[128,128]{1,0:T(8,128)(2,1)S(1)}, bf16[128,128]{1,0:T(8,128)(2,1)S(1)}, u32[]{:S(2)}, u32[]{:S(2)}) collective-permute-start(bf16[128,128]{1,0:T(8,128)(2,1)S(1)} %slice.62), channel_id=1, source_target_pairs={{0,8},{8,16},{16,24},{24,32},{32,40},{40,48},{48,56},{56,64},{64,7... | collective-permute-start | bytes 98312 | tf_op jit(solution)/shard_map/ppermute | solution.py:345
  44.8 1.6 copy-start.10
  44.8 2.4 copy-start.11
  44.8 3.1 copy-start.3
  49.0 2.6 slice-start
  52.2 0.8 copy-start.4
  258.1 2.1 copy-start.5
  261.0 32.9 %collective-permute-start.1 = (bf16[128,128]{0,1:T(8,128)(2,1)S(1)}, bf16[128,128]{0,1:T(8,128)(2,1)S(1)}, u32[]{:S(2)}, u32[]{:S(2)}) collective-permute-start(bf16[128,128]{0,1:T(8,128)(2,1)S(1)} %fusion.32), channel_id=1, source_target_pairs={{8,0},{16,8},{24,16},{32,24},{40,32},{48,40},{56,48},{64,56},{72,6... | collective-permute-start | bytes 98312 | tf_op jit(solution)/shard_map/ppermute | solution.py:345
  350.4 33.9 %copy-start.2 = (bf16[2880,256]{1,0:T(8,128)(2,1)S(1)}, bf16[2880,256]{1,0:T(8,128)(2,1)}, u32[]{:S(2)}) copy-start(bf16[2880,256]{1,0:T(8,128)(2,1)} %get-tuple-element.19) | copy-start | bytes 4423684
  384.3 1.9 copy-start.1

commit v3 on v2

--- a/solution.py
+++ b/solution.py
@@ -126,13 +126,7 @@
     return v.astype(jnp.bfloat16)
 
 
-def scatter_kernel(t_ref, out_ref, far, near, stage, acc1, far2, near2, stage2, acc2, last, send, recv):
-    c, z, y, x = place()
-    e = lax.axis_index(EXP)
-
-    def dev(zz, yy, xx):
-        return (zz * 16 + ((yy + 4) % 4) * 4 + (xx + 4) % 4, e)
-
+def copier(send, recv):
     def copy(n, src, dst, to):
         cp = pltpu.make_async_remote_copy(
             src_ref=src, dst_ref=dst, send_sem=send.at[n], recv_sem=recv.at[n],
@@ -141,7 +135,27 @@
         cp.start()
         return cp
 
-    greet([dev(1 - z, y, x), dev(z, y + 1, x), dev(z, y - 1, x), dev(z, y, x + 1), dev(z, y, x - 1)])
+    return copy
+
+
+def take_turns(*parts):
+    running = list(parts)
+    while running:
+        for part in list(running):
+            try:
+                next(part)
+            except StopIteration:
+                running.remove(part)
+
+
+def scatter_steps(t_ref, out_ref, far, near, stage, acc1, far2, near2, stage2, acc2, last, send, recv):
+    c, z, y, x = place()
+    e = lax.axis_index(EXP)
+    copy = copier(send, recv)
+
+    def dev(zz, yy, xx):
+        return (zz * 16 + ((yy + 4) % 4) * 4 + (xx + 4) % 4, e)
+
     rows = (pl.ds(0, 48), pl.ds(48, 48))
     copies = []
 
@@ -151,7 +165,17 @@
         down = dev(z, y, x - 1) if along_x else dev(z, y - 1, x)
         return me, (me + 3) % 4, (me + 1) % 4, (me + 2) % 4, up, down
 
-    def step(phase, source, far_ref, near_ref, stage_ref):
+    def first_source(h, zsel, pos):
+        return t_ref.at[zsel, pos, :, rows[h]] if h == 0 else t_ref.at[zsel, :, pos, rows[h]]
+
+    def second_source(h, zsel, pos):
+        return acc1.at[h, zsel, pos]
+
+    final = []
+    for phase, source, far_ref, near_ref, stage_ref, acc in (
+        (1, first_source, far, near, stage, acc1),
+        (2, second_source, far2, near2, stage2, acc2),
+    ):
         started = []
         for h in range(2):
             me, low, high, across, up, down = ring((h == 1) == (phase == 1))
@@ -162,6 +186,7 @@
                 copy(n + 2, source(h, 1, high), near_ref.at[h, 0, 1], up),
                 copy(n + 3, source(h, 0, low), near_ref.at[h, 1, 0], down),
             ])
+        yield
         for h in range(2):
             me, low, high, across, up, down = ring((h == 1) == (phase == 1))
             n = (phase - 1) * 12 + h * 6
@@ -171,33 +196,19 @@
             started[h][1].wait_recv()
             stage_ref[h, 1] = bf(f32(source(h, 1, low)[...]) + f32(far_ref[h, 1]))
             started[h].append(copy(n + 5, stage_ref.at[h, 1], near_ref.at[h, 1, 1], down))
-        return started
-
-    def first_source(h, zsel, pos):
-        return t_ref.at[zsel, pos, :, rows[h]] if h == 0 else t_ref.at[zsel, :, pos, rows[h]]
-
-    started = step(1, first_source, far, near, stage)
-    for h in range(2):
-        me = ring(h == 1)[0]
-        for i in (2, 3, 4, 5):
-            started[h][i].wait_recv()
-        for zz in range(2):
-            acc1[h, zz] = bf(f32(first_source(h, zz, me)[...]) + f32(near[h, 0, zz]) + f32(near[h, 1, zz]))
-        copies += started[h]
-
-    def second_source(h, zsel, pos):
-        return acc1.at[h, zsel, pos]
-
-    started = step(2, second_source, far2, near2, stage2)
-    final = []
-    for h in range(2):
-        me = ring(h == 0)[0]
-        for i in (2, 3, 4, 5):
-            started[h][i].wait_recv()
-        for zz in range(2):
-            acc2[h, zz] = bf(f32(second_source(h, zz, me)[...]) + f32(near2[h, 0, zz]) + f32(near2[h, 1, zz]))
-        copies += started[h]
-        final.append(copy(24 + h, acc2.at[h, 1 - z], last.at[h], dev(1 - z, y, x)))
+        yield
+        for h in range(2):
+            me = ring((h == 1) == (phase == 1))[0]
+            for i in (2, 3, 4, 5):
+                started[h][i].wait_recv()
+            for zz in range(2):
+                acc[h, zz] = bf(
+                    f32(source(h, zz, me)[...]) + f32(near_ref[h, 0, zz]) + f32(near_ref[h, 1, zz])
+                )
+            copies += started[h]
+            if phase == 2:
+                final.append(copy(24 + h, acc2.at[h, 1 - z], last.at[h], dev(1 - z, y, x)))
+    yield
     for h in range(2):
         final[h].wait_recv()
         out_ref[rows[h], :] = bf(f32(acc2[h, z]) + f32(last[h]))
@@ -205,107 +216,265 @@
         cp.wait_send()
 
 
-def scatter_sums(terms):
+def scatter_scratch():
     b = jnp.bfloat16
-    return pl.pallas_call(
-        scatter_kernel,
-        out_shape=jax.ShapeDtypeStruct((PADDED, 640), b),
-        in_specs=vmem_specs(1),
-        out_specs=vmem_specs(1)[0],
-        scratch_shapes=[
-            pltpu.VMEM((2, 2, 4, 48, 640), b),
-            pltpu.VMEM((2, 2, 2, 4, 48, 640), b),
-            pltpu.VMEM((2, 2, 4, 48, 640), b),
-            pltpu.VMEM((2, 2, 4, 48, 640), b),
-            pltpu.VMEM((2, 2, 48, 640), b),
-            pltpu.VMEM((2, 2, 2, 48, 640), b),
-            pltpu.VMEM((2, 2, 48, 640), b),
-            pltpu.VMEM((2, 2, 48, 640), b),
-            pltpu.VMEM((2, 48, 640), b),
-            pltpu.SemaphoreType.DMA((26,)),
-            pltpu.SemaphoreType.DMA((26,)),
-        ],
-        compiler_params=params(1),
-        name="scatter_sums",
-    )(terms.reshape(2, 4, 4, PADDED, 640))
-
-
-def sum_kernel(post, extra_in, extra_out, *refs):
-    part = refs[0]
-    ins = refs[1 : 1 + extra_in]
-    out = refs[1 + extra_in]
-    outs = refs[2 + extra_in : 2 + extra_in + extra_out]
-    mate, stage, got, send, recv = refs[2 + extra_in + extra_out :]
+    return [
+        pltpu.VMEM((2, 2, 4, 48, 640), b),
+        pltpu.VMEM((2, 2, 2, 4, 48, 640), b),
+        pltpu.VMEM((2, 2, 4, 48, 640), b),
+        pltpu.VMEM((2, 2, 4, 48, 640), b),
+        pltpu.VMEM((2, 2, 48, 640), b),
+        pltpu.VMEM((2, 2, 2, 48, 640), b),
+        pltpu.VMEM((2, 2, 48, 640), b),
+        pltpu.VMEM((2, 2, 48, 640), b),
+        pltpu.VMEM((2, 48, 640), b),
+        pltpu.SemaphoreType.DMA((26,)),
+        pltpu.SemaphoreType.DMA((26,)),
+    ]
+
+
+def exp_peers():
     c = lax.axis_index(CTX)
     e = lax.axis_index(EXP)
     h, k = e // 2, e % 2
-    partner = (c, e + 1 - 2 * k)
-
-    def peer(d):
-        return (c, ((h + d) % 4) * 2 + k)
-
-    greet([partner, peer(1), peer(2), peer(3)])
+    return (c, e + 1 - 2 * k), (c, ((h + 1) % 4) * 2 + k), (c, ((h + 3) % 4) * 2 + k)
+
+
+def sum_steps(post, part, out, mate, stage, far, near, send, recv):
+    e = lax.axis_index(EXP)
+    h, k = e // 2, e % 2
+    partner, up, down = exp_peers()
+    copy = copier(send, recv)
+    lanes = (pl.ds(0, 1408), pl.ds(1408, MODEL - 1408))
 
     def rows(core, block):
         return pl.ds(pl.multiple_of(core * 64 + block * 16, 16), 16)
 
-    def copy(n, src, dst, to):
-        cp = pltpu.make_async_remote_copy(
-            src_ref=src, dst_ref=dst, send_sem=send.at[n], recv_sem=recv.at[n],
-            device_id=to, device_id_type=MESH,
-        )
-        cp.start()
-        return cp
-
-    order = (2, 1, 3, 0)
-    copies, pair, far = [], {}, {}
-    for d in order:
-        b = (h + d) % 4
-        pair[d] = copy(d, part.at[rows(1 - k, b)], mate.at[b], partner)
-    for d in order:
-        b = (h + d) % 4
-        pair[d].wait_recv()
-        both = f32(part[rows(k, b), :]) + f32(mate[b])
-        if d:
-            stage[d - 1] = bf(both)
-            far[d] = copy(4 + d, stage.at[d - 1], got.at[d - 1], peer(d))
-    total = both
-    for d in (1, 3, 2):
-        far[d].wait_recv()
-        total = total + f32(got[d - 1])
+    high, low, across = (h + 1) % 4, (h + 3) % 4, (h + 2) % 4
+    order = (across, high, low, h)
+    pair = [copy(i, part.at[rows(1 - k, b)], mate.at[b], partner) for i, b in enumerate(order)]
+    yield
+    pair[0].wait_recv()
+    stage[across] = bf(f32(part[rows(k, across), :]) + f32(mate[across]))
+    copies = [
+        copy(4, stage.at[across, :, lanes[0]], far.at[:, lanes[0]], up),
+        copy(5, stage.at[across, :, lanes[1]], far.at[:, lanes[1]], down),
+    ]
+    pair[1].wait_recv()
+    stage[high] = bf(f32(part[rows(k, high), :]) + f32(mate[high]))
+    copies.append(copy(6, stage.at[high, :, lanes[1]], near.at[0, :, lanes[1]], up))
+    pair[2].wait_recv()
+    stage[low] = bf(f32(part[rows(k, low), :]) + f32(mate[low]))
+    copies.append(copy(7, stage.at[low, :, lanes[0]], near.at[1, :, lanes[0]], down))
+    yield
+    copies[0].wait_recv()
+    stage[high, :, lanes[0]] = bf(f32(stage[high, :, lanes[0]]) + f32(far[:, lanes[0]]))
+    copies.append(copy(8, stage.at[high, :, lanes[0]], near.at[0, :, lanes[0]], up))
+    copies[1].wait_recv()
+    stage[low, :, lanes[1]] = bf(f32(stage[low, :, lanes[1]]) + f32(far[:, lanes[1]]))
+    copies.append(copy(9, stage.at[low, :, lanes[1]], near.at[1, :, lanes[1]], down))
+    pair[3].wait_recv()
+    total = f32(part[rows(k, h), :]) + f32(mate[h])
+    yield
+    for cp in copies[2:]:
+        cp.wait_recv()
     mine = rows(k, h)
-    out[mine, :] = post(total, mine, *ins, *outs)
-    spread = {d: copy(8 + d, out.at[mine], out.at[mine], peer(d)) for d in (2, 1, 3)}
+    out[mine, :] = post(total + f32(near[0]) + f32(near[1]), mine)
+    direct = [copy(10, out.at[mine], out.at[mine], up), copy(11, out.at[mine], out.at[mine], down)]
     passed = [copy(12, out.at[mine], out.at[mine], partner)]
-    for d in (1, 3, 2):
-        spread[d].wait_recv()
-        theirs = rows(k, (h - d + 4) % 4)
-        passed.append(copy(12 + d, out.at[theirs], out.at[theirs], partner))
+    yield
+    theirs = rows(k, low), rows(k, high)
+    for i, to in enumerate((up, down)):
+        direct[i].wait_recv()
+        view = out.at[theirs[i], lanes[i]]
+        direct.append(copy(13 + i, view, view, to))
+    for i in range(2):
+        passed.append(copy(15 + i, out.at[theirs[i]], out.at[theirs[i]], partner))
+    yield
+    for i in range(2):
+        direct[2 + i].wait_recv()
+        view = out.at[rows(k, across), lanes[i]]
+        passed.append(copy(17 + i, view, view, partner))
+    yield
     for cp in passed:
         cp.wait_recv()
-    for cp in [*pair.values(), *far.values(), *spread.values(), *passed]:
+    for cp in [*pair, *copies, *direct, *passed]:
         cp.wait_send()
 
 
-def sum_heads(part, post, ins, collective_id, extra_outs=(), name="sum_heads"):
+def sum_scratch():
     b = jnp.bfloat16
-    width = part.shape[1]
-    res = pl.pallas_call(
-        functools.partial(sum_kernel, post, len(ins), len(extra_outs)),
-        out_shape=[jax.ShapeDtypeStruct((128, width), b), *extra_outs],
-        in_specs=vmem_specs(1 + len(ins)),
-        out_specs=vmem_specs(1 + len(extra_outs)),
+    return [
+        pltpu.VMEM((4, 16, MODEL), b),
+        pltpu.VMEM((4, 16, MODEL), b),
+        pltpu.VMEM((16, MODEL), b),
+        pltpu.VMEM((2, 16, MODEL), b),
+        pltpu.SemaphoreType.DMA((20,)),
+        pltpu.SemaphoreType.DMA((20,)),
+    ]
+
+
+def ring_ctx():
+    c = lax.axis_index(CTX)
+    e = lax.axis_index(EXP)
+    return ((c + 1) % 32, e), ((c + 31) % 32, e)
+
+
+def drop_into(ref, values):
+    for i in range(32):
+        ref[:, SHARD * i : SHARD * (i + 1)] = values[:, PADDED * i : PADDED * i + SHARD]
+
+
+def attention_kernel(
+    normed_pad, full, tokens, residual, projected, span, attended, prob_ref, part, rim_send, rim_recv, *scratch
+):
+    c = lax.axis_index(CTX)
+    after, before = ring_ctx()
+    greet([*exp_peers(), after, before])
+    made = bf(dot(normed_pad[...], full[:, :384]))
+    projected[...] = made
+    span[128:, :] = made[:, 256:]
+    rim = copier(rim_send, rim_recv)(0, span.at[pl.ds(128, 128)], span.at[pl.ds(0, 128)], after)
+    query_pos, key_pos = iota((128, 256), 0), iota((128, 256), 1)
+    valid = (key_pos <= query_pos + 128) & (key_pos > query_pos) & (key_pos + c * 128 >= 128)
+    rim.wait_recv()
+    keys, values = span[:, :HEAD_SIZE], span[:, HEAD_SIZE:]
+    for h in range(GROUP):
+        scores = dot_nt(made[:, HEAD_SIZE * h : HEAD_SIZE * (h + 1)], keys) * 0.125
+        weights = jnp.where(valid, jnp.exp(scores), 0.0)
+        prob = weights / jnp.sum(weights, axis=-1, keepdims=True)
+        prob_ref[h] = prob
+        attended[:, HEAD_SIZE * h : HEAD_SIZE * (h + 1)] = bf(dot(bf(prob), values))
+    drop_into(part, bf(dot_nt(attended[...], full[:, 384:])))
+    rim.wait_send()
+    take_turns(sum_steps(lambda t, m: add_base(t, m, tokens), part, residual, *scratch))
+
+
+def attention(normed_pad, full, tokens):
+    b = jnp.bfloat16
+    shape = jax.ShapeDtypeStruct
+    return pl.pallas_call(
+        attention_kernel,
+        out_shape=[
+            shape((128, MODEL), b), shape((128, 384), b), shape((256, 128), b), shape((128, 256), b),
+            shape((4, 128, 256), jnp.float32),
+        ],
+        in_specs=vmem_specs(3),
+        out_specs=vmem_specs(5),
         scratch_shapes=[
-            pltpu.VMEM((4, 16, width), b),
-            pltpu.VMEM((3, 16, width), b),
-            pltpu.VMEM((3, 16, width), b),
-            pltpu.SemaphoreType.DMA((16,)),
-            pltpu.SemaphoreType.DMA((16,)),
+            pltpu.VMEM((128, MODEL), b), pltpu.SemaphoreType.DMA((1,)), pltpu.SemaphoreType.DMA((1,)),
+        ] + sum_scratch(),
+        compiler_params=params(1),
+        name="attention",
+    )(normed_pad, full, tokens)
+
+
+def grad_residual_kernel(part, cotangent, residual, out, own, *scratch):
+    greet(exp_peers())
+    take_turns(sum_steps(lambda t, m: finish_resid(t, m, cotangent, residual, own), part, out, *scratch))
+
+
+def grad_residual(part, cotangent, residual):
+    return pl.pallas_call(
+        grad_residual_kernel,
+        out_shape=[
+            jax.ShapeDtypeStruct((128, MODEL), jnp.bfloat16),
+            jax.ShapeDtypeStruct((16, MODEL), jnp.float32),
         ],
-        compiler_params=params(collective_id),
-        name=name,
-    )(part, *ins)
-    return res
+        in_specs=vmem_specs(3),
+        out_specs=vmem_specs(2),
+        scratch_shapes=sum_scratch(),
+        compiler_params=params(3),
+        name="grad_residual",
+    )(part, cotangent, residual)
+
+
+def last_kernel(
+    moe_part, residual, tokens, grad_resid, grad_resid_bf, normed_pad, full, projected, span, attended, prob_ref,
+    block_out, grad_tokens, sums,
+    resid_pad, qkv_grad, rim_out, rim_in, grad_part, terms, rim_send, rim_recv, *scratch
+):
+    c, z, y, x = place()
+    e = lax.axis_index(EXP)
+    after, before = ring_ctx()
+    near = [
+        ((1 - z) * 16 + y * 4 + x, e),
+        (z * 16 + (y + 1) % 4 * 4 + x, e),
+        (z * 16 + (y + 3) % 4 * 4 + x, e),
+        (z * 16 + y * 4 + (x + 1) % 4, e),
+        (z * 16 + y * 4 + (x + 3) % 4, e),
+    ]
+    greet([*near, *exp_peers(), after, before])
+    block_sum = sum_steps(lambda t, m: add_base(t, m, residual), moe_part, block_out, *scratch[6:12])
+    next(block_sum)
+
+    resid_pad[...] = jnp.zeros_like(resid_pad)
+    for i in range(32):
+        resid_pad[:, PADDED * i : PADDED * i + SHARD] = grad_resid_bf[:, SHARD * i : SHARD * (i + 1)]
+    attended_grad = bf(dot(resid_pad[...], full[:, 384:]))
+    keys, values = span[:, :HEAD_SIZE], span[:, HEAD_SIZE:]
+    grad_key = jnp.zeros((256, HEAD_SIZE), jnp.float32)
+    grad_value = jnp.zeros((256, HEAD_SIZE), jnp.float32)
+    for h in range(GROUP):
+        head = pl.ds(HEAD_SIZE * h, HEAD_SIZE)
+        grad_out = attended_grad[:, HEAD_SIZE * h : HEAD_SIZE * (h + 1)]
+        prob = prob_ref[h]
+        grad_prob = dot_nt(grad_out, values)
+        grad_value = grad_value + dot_tn(bf(prob), grad_out)
+        inner = jnp.sum(grad_prob * prob, axis=-1, keepdims=True)
+        grad_score = bf(prob * (grad_prob - inner) * 0.125)
+        qkv_grad[:, head] = bf(dot(grad_score, keys))
+        grad_key = grad_key + dot_tn(grad_score, projected[:, head])
+    rim_out[:, :HEAD_SIZE] = bf(grad_key[:128])
+    rim_out[:, HEAD_SIZE:] = bf(grad_value[:128])
+    rim = copier(rim_send, rim_recv)(0, rim_out, rim_in, before)
+
+    def term(left, right, columns):
+        def four(i, t):
+            rows = left[:, pl.ds(pl.multiple_of(i * 384, 128), 384)]
+            terms[i // 4, i % 4, :, :, columns] = bf(dot_tn(rows, right)).reshape(4, PADDED, columns.size)
+            return t
+
+        lax.fori_loop(0, 8, four, 0)
+
+    term(resid_pad, attended[...], pl.ds(384, 256))
+    next(block_sum)
+    rim.wait()
+    qkv_grad[:, 256:320] = bf(grad_key[128:] + f32(rim_in[:, :HEAD_SIZE]))
+    qkv_grad[:, 320:] = bf(grad_value[128:] + f32(rim_in[:, HEAD_SIZE:]))
+    grads = qkv_grad[...]
+    drop_into(grad_part, bf(dot_nt(grads, full[:, :384])))
+    token_sum = sum_steps(
+        lambda t, m: finish_tokens(t, m, tokens, grad_resid), grad_part, grad_tokens, *scratch[:6]
+    )
+    next(token_sum)
+    term(normed_pad, grads, pl.ds(0, 384))
+    take_turns(scatter_steps(terms, sums, *scratch[12:]), token_sum, block_sum)
+
+
+def last_sums(*operands):
+    b = jnp.bfloat16
+    return pl.pallas_call(
+        last_kernel,
+        out_shape=[
+            jax.ShapeDtypeStruct((128, MODEL), b), jax.ShapeDtypeStruct((128, MODEL), b),
+            jax.ShapeDtypeStruct((PADDED, 640), b),
+        ],
+        in_specs=vmem_specs(11),
+        out_specs=vmem_specs(3),
+        scratch_shapes=[
+            pltpu.VMEM((128, 32 * PADDED), b),
+            pltpu.VMEM((128, 384), b),
+            pltpu.VMEM((128, 128), b),
+            pltpu.VMEM((128, 128), b),
+            pltpu.VMEM((128, MODEL), b),
+            pltpu.VMEM((2, 4, 4, PADDED, 640), b),
+            pltpu.SemaphoreType.DMA((1,)),
+            pltpu.SemaphoreType.DMA((1,)),
+        ] + sum_scratch() + sum_scratch() + scatter_scratch(),
+        compiler_params=params(4),
+        name="last_sums",
+    )(*operands)
 
 
 EPSILON = 1e-05
@@ -339,49 +508,8 @@
     return inv_rms * grad_in - values * (inv_rms * inv_rms * inv_rms) * inner_mean
 
 
-def shifted(shard, by):
-    size = lax.axis_size(CTX)
-    pairs = [(i, i + by) for i in range(size) if 0 <= i + by < size]
-    return lax.ppermute(shard, CTX, pairs)
-
-
 def pad_features(v):
     return jnp.pad(v.reshape(-1, 32, SHARD), ((0, 0), (0, 0), (0, PADDED - SHARD))).reshape(-1, 32 * PADDED)
-
-
-def drop_padding(v):
-    return v.reshape(-1, 32, PADDED)[:, :, :SHARD].reshape(-1, MODEL)
-
-
-def band_valid(block_idx):
-    query_pos = block_idx * 128 + jnp.arange(128)[:, None]
-    key_pos = block_idx * 128 - WINDOW + jnp.arange(WINDOW + 128)[None, :]
-    return (key_pos <= query_pos) & (key_pos > query_pos - WINDOW) & (key_pos >= 0)
-
-
-def attend(query, keys, values, valid):
-    scores = dot_nt(query, keys) * 0.125
-    weights = jnp.where(valid, jnp.exp(scores), 0.0)
-    prob = weights / jnp.sum(weights, axis=-1, keepdims=True)
-    prob_bf = bf(prob)
-    return bf(dot(prob_bf, values)), prob, prob_bf
-
-
-def attend_back(query, keys, values, prob, prob_bf, grad_out):
-    grad_prob = dot_nt(grad_out, values)
-    grad_value = dot_tn(prob_bf, grad_out)
-    grad_score = bf(
-        prob * (grad_prob - jnp.sum(grad_prob * prob, axis=-1, keepdims=True)) * 0.125
-    )
-    return dot(grad_score, keys), dot_tn(grad_score, query), grad_value
-
-
-def heads_first(v):
-    return v.reshape(128, GROUP, HEAD_SIZE).transpose(1, 0, 2).reshape(GROUP * 128, HEAD_SIZE)
-
-
-def heads_last(v):
-    return v.reshape(GROUP, 128, HEAD_SIZE).transpose(1, 0, 2).reshape(128, GROUP * HEAD_SIZE)
 
 
 def iota(shape, axis):
@@ -433,8 +561,9 @@
         extra_hot[q] = bf(jnp.where(extra & (lane % 16 // 4 == q), 1.0, 0.0))
     scale[0] = jnp.sum(jnp.where(main, weight, 0.0).T, axis=1, keepdims=True)
     scale[1] = jnp.sum(jnp.where(extra, weight, 0.0).T, axis=1, keepdims=True)
-    for a, ref in enumerate((x_ref, cot_ref)):
-        xp[a, :, :MODEL] = ref[...]
+    res = f32(x_ref[...])
+    for a, rows in enumerate((bf(res * inverse_rms(res)), cot_ref[...])):
+        xp[a, :, :MODEL] = rows
         xp[a, :, MODEL:] = jnp.zeros((128, 192), jnp.bfloat16)
 
     def out_copy(a, n):
@@ -654,7 +783,7 @@
         lax.fori_loop(0, 4, lambda j, t, a=a: (across(a, j).wait_send(), t)[1], 0)
 
 
-def experts(moe_input, cotangent, expert_ids, combine_weights, w_gate, w_up, w_down):
+def experts(residual, cotangent, expert_ids, combine_weights, w_gate, w_up, w_down):
     b = jnp.bfloat16
     shape = jax.ShapeDtypeStruct
     return pl.pallas_call(
@@ -686,7 +815,7 @@
         + [pltpu.SemaphoreType.DMA((2, 4))] * 2 + [pltpu.SemaphoreType.DMA((2, 32))] * 2,
         compiler_params=params(2),
         name="experts",
-    )(moe_input, cotangent, expert_ids, combine_weights, w_gate, w_up, w_down)
+    )(residual, cotangent, expert_ids, combine_weights, w_gate, w_up, w_down)
 
 
 def add_base(total, mine, base):
@@ -709,48 +838,21 @@
     tokens, cotangent, expert_ids, combine_weights,
     w_query, key_value_weight, w_output, w_gate, w_up, w_down,
 ):
-    ctx_block = lax.axis_index(CTX)
     tokens_f32 = f32(tokens)
     normed = bf(tokens_f32 * inverse_rms(tokens_f32))
     normed_pad = pad_features(normed)
     shard = jnp.concatenate([w_query, key_value_weight, w_output.T], axis=1)
     full = gather_weights(jnp.pad(shard, ((0, PADDED - SHARD), (0, 0))))
 
-    projected = bf(dot(normed_pad, full[:, :384]))
-    query_matrix, key_value = projected[:, :256], projected[:, 256:]
-    prev_rim = shifted(key_value, 1)
-    span = jnp.concatenate([prev_rim, key_value], axis=0)
-    keys, values = span[:, :HEAD_SIZE], span[:, HEAD_SIZE:]
-    valid = jnp.tile(band_valid(ctx_block), (GROUP, 1))
-    query = heads_first(query_matrix)
-    attended, prob, prob_bf = attend(query, keys, values, valid)
-    attended = heads_last(attended)
-    head_part = bf(drop_padding(dot_nt(attended, full[:, 384:])))
-    (residual,) = sum_heads(head_part, add_base, [tokens], 4, name="residual")
-    residual_f32 = f32(residual)
-    moe_input = bf(residual_f32 * inverse_rms(residual_f32))
-    grad_normed, moe_part, grad_gate, grad_up, grad_down = experts(
-        moe_input, cotangent, expert_ids, combine_weights, w_gate[0], w_up[0], w_down[0]
+    residual, projected, span, attended, prob = attention(normed_pad, full, tokens)
+    grad_in_part, moe_part, grad_gate, grad_up, grad_down = experts(
+        residual, cotangent, expert_ids, combine_weights, w_gate[0], w_up[0], w_down[0]
     )
-    own = jax.ShapeDtypeStruct((16, MODEL), jnp.float32)
-    grad_resid_bf, grad_resid = sum_heads(
-        grad_normed, finish_resid, [cotangent, residual], 5, (own,), name="grad_residual"
+    grad_resid_bf, grad_resid = grad_residual(grad_in_part, cotangent, residual)
+    block_out, grad_tokens, sums = last_sums(
+        moe_part, residual, tokens, grad_resid, grad_resid_bf, normed_pad, full, projected, span, attended, prob
     )
-    (block_out,) = sum_heads(moe_part, add_base, [residual], 4, name="block_out")
-    resid_pad = pad_features(grad_resid_bf)
-    attended_grad = bf(dot(resid_pad, full[:, 384:]))
-    query_grads, key_grads, value_grads = attend_back(
-        query, keys, values, prob, prob_bf, heads_first(attended_grad)
-    )
-    span_grads = jnp.concatenate([key_grads, value_grads], axis=1)
-    rim_grad = f32(shifted(bf(span_grads[:WINDOW]), -1))
-    key_value_grad = bf(span_grads[WINDOW:] + rim_grad)
-    query_grad = heads_last(bf(query_grads))
-    qkv_grad = jnp.concatenate([query_grad, key_value_grad], axis=1)
-    grad_part = bf(drop_padding(dot_nt(qkv_grad, full[:, :384])))
-    (grad_tokens,) = sum_heads(grad_part, finish_tokens, [tokens, grad_resid], 6, name="grad_tokens")
-    terms = bf(jnp.concatenate([dot_tn(normed_pad, qkv_grad), dot_tn(resid_pad, attended)], axis=1))
-    sums = scatter_sums(terms)[:SHARD]
+    sums = sums[:SHARD]
     return (
         block_out, grad_tokens, sums[:, :256], sums[:, 256:384], sums[:, 384:].T,
         grad_gate[None], grad_up[None], grad_down[None],

time: 388 us -> 317 us (0.82)
  Pallas kernels: 335 us -> 296 us
  matrix products: 10.2 us -> 0 us
  local copies, waits for them, and re-layouts: 27 us -> 17.7 us
  other arithmetic: 9.69 us -> 3.24 us
  starting transfers between devices: 4.46 us -> 0 us
    pallas_call x5 -> x3, Pallas kernels: 163 us -> 129 us  [the longest x1 57.3 us: last_sums(): pl.pallas_call(last_kernel, out_shape=[jax.ShapeDtypeStruct((128, MODEL),...]
    dot_general x12 -> x0, matrix products: 10.2 us -> none  [the longest x4 4.76 us: dot(): return jnp.dot(a, b, preferred_element_type=jnp.float32)]
    pallas_call x1, Pallas kernels: 138 us -> 133 us  [experts(): pl.pallas_call(expert_kernel, out_shape=[shape((128, MODEL), b), shape((1...]
    ppermute x2 -> x0, starting transfers between devices: 4.46 us -> none  [shifted(): return lax.ppermute(shard, CTX, pairs)]
    unnamed x34 -> x26, local copies, waits for them, and re-layouts: 17 us -> 15 us
  transfers between devices with their start and end apart: 2 -> 0, of which waited for: 0 -> 0; matrix products, arithmetic and copies ran while one was open for 4% -> 0% of each run, Pallas kernels for 7% -> 0%
where the time goes in v3:
time: 317 us
  Pallas kernels  296 us (93%)
  local copies, waits for them, and re-layouts  17.7 us (6%)
  other arithmetic  3.24 us (1%)
    pallas_call x1, Pallas kernels, experts(): pl.pallas_call(expert_kernel, out_shape=[shape((128, MODEL), b), shape((1...  133 us
    pallas_call x1, Pallas kernels, last_sums(): pl.pallas_call(last_kernel, out_shape=[jax.ShapeDtypeStruct((128, MODEL),...  57.3 us
    pallas_call x1, Pallas kernels, attention(): pl.pallas_call(attention_kernel, out_shape=[shape((128, MODEL), b), shape...  44.8 us
    pallas_call x1, Pallas kernels, gather_weights(): pl.pallas_call(gather_kernel, out_shape=jax.ShapeDtypeStruct((2, 4, 4, PA...  33.7 us
    pallas_call x1, Pallas kernels, grad_residual(): pl.pallas_call(grad_residual_kernel, out_shape=[jax.ShapeDtypeStruct((128...  27 us
    unnamed x26, local copies, waits for them, and re-layouts  15 us

profile of v3, /device:TPU:1, one launch (start us, length us, event | category | flops | bytes accessed | tf_op | source)
XLA Modules:
  0.0 317.2 jit_solution(11967164678350015754)
XLA Ops:
  0.6 1.6 fusion
  2.2 1.4 copy.33.ids_ref
  3.7 1.4 copy.34.combine_ref
  5.1 1.5 fusion.6.w_ref
  6.6 0.1 fusion.1
  6.7 0.2 reshape.33
  6.9 0.1 pad.8
  7.0 1.2 copy.29.normed_pad
  8.2 1.2 copy.32.cot_ref.cotangent
  9.3 1.2 copy.30.tokens
  10.5 1.7 copy.31
  12.2 33.7 %gather_weights.1 = bf16[2,4,4,96,640]{4,3,2,1,0:T(8,128)(2,1)} custom-call(bf16[96,640]{1,0:T(8,128)(2,1)} %fusion.6.w_ref), custom_call_target="tpu_custom_call" | custom-call | tf_op jit(solution)/shard_map/gather_weights/pallas_call | solution.py:109
  45.9 44.8 %attention.1 = (bf16[128,2880]{1,0:T(8,128)(2,1)}, bf16[128,384]{1,0:T(8,128)(2,1)}, bf16[256,128]{1,0:T(8,128)(2,1)}, bf16[128,256]{1,0:T(8,128)(2,1)}, f32[4,128,256]{2,1,0:T(8,128)}) custom-call(bf16[128,3072]{1,0:T(8,128)(2,1)} %copy.29.normed_pad, bf16[3072,640]{1,0:T(8,128)(2,1)} %bitcast.13, bf16[128,2880]{1,0:T(8,128)(2,1)} %copy.30.tokens), custom_call_target="tpu_custom_call" | custom-call | tf_op jit(solution)/shard_map/attention/pallas_call | solution.py:356
  90.8 132.7 %experts.1 = (bf16[128,2880]{1,0:T(8,128)(2,1)}, bf16[128,2880]{1,0:T(8,128)(2,1)}, bf16[2880,256]{1,0:T(8,128)(2,1)}, bf16[2880,256]{1,0:T(8,128)(2,1)}, bf16[256,2880]{1,0:T(8,128)(2,1)}) custom-call(bf16[128,2880]{1,0:T(8,128)(2,1)} %get-tuple-element.23.x_ref.residual, bf16[128,2880]{1,0:T(8,128)(2,1)} %copy.32.cot_ref.cotangent, ...), custom_call_target="tpu_custom_call" | custom-call | tf_op jit(solution)/shard_map/experts/pallas_call | solution.py:789
  223.4 27.0 %grad_residual.1 = (bf16[128,2880]{1,0:T(8,128)(2,1)}, f32[16,2880]{1,0:T(8,128)}) custom-call(bf16[128,2880]{1,0:T(8,128)(2,1)} %get-tuple-element.25.part, bf16[128,2880]{1,0:T(8,128)(2,1)} %copy.32.cot_ref.cotangent, bf16[128,2880]{1,0:T(8,128)(2,1)} %get-tuple-element.23.x_ref.residual), custom_call_target="tpu_custom_call" | custom-call | tf_op jit(solution)/shard_map/grad_residual/pallas_call | solution.py:378
  250.4 57.3 %last_sums.1 = (bf16[128,2880]{1,0:T(8,128)(2,1)}, bf16[128,2880]{1,0:T(8,128)(2,1)}, bf16[96,640]{1,0:T(8,128)(2,1)}) custom-call(bf16[128,2880]{1,0:T(8,128)(2,1)} %get-tuple-element.24.moe_part, bf16[128,2880]{1,0:T(8,128)(2,1)} %get-tuple-element.23.x_ref.residual, bf16[128,2880]{1,0:T(8,128)(2,1)} %copy.30.tokens, ...), custom_call_target="tpu_custom_call" | custom-call | tf_op jit(solution)/shard_map/last_sums/pallas_call | solution.py:457
  307.8 2.4 copy.38
  310.2 0.6 slice.14
  310.8 0.6 slice_bitcast_fusion
  311.5 1.1 copy.39
  312.6 1.5 copy.40
  314.1 1.1 copy.43
  315.3 0.8 copy-done.3
  316.1 1.1 copy.44
  (16 shorter events, 0.0 us)
Async XLA Ops:
  0.6 5.9 %copy-start = (bf16[128,2880]{0,1:T(8,128)(2,1)S(1)}, bf16[128,2880]{0,1:T(8,128)(2,1)}, u32[]{:S(2)}) copy-start(bf16[128,2880]{0,1:T(8,128)(2,1)} %param.10) | copy-start | bytes 2211844
  6.9 1.3 copy-start.6
  8.2 2.3 copy-start.2
  307.8 2.4 copy-start.7
  307.8 3.7 %copy-start.5 = (bf16[128,2880]{1,0:T(8,128)(2,1)S(1)}, bf16[128,2880]{1,0:T(8,128)(2,1)}, u32[]{:S(2)}) copy-start(bf16[128,2880]{1,0:T(8,128)(2,1)} %get-tuple-element.47) | copy-start | bytes 2211844
  307.8 4.8 %copy-start.1 = (bf16[256,2880]{1,0:T(8,128)(2,1)S(1)}, bf16[256,2880]{1,0:T(8,128)(2,1)}, u32[]{:S(2)}) copy-start(bf16[256,2880]{1,0:T(8,128)(2,1)} %get-tuple-element.37) | copy-start | bytes 4423684
  312.6 1.5 copy-start.4
  314.1 1.9 copy-start.3

commit v4 on v3

--- a/solution.py
+++ b/solution.py
@@ -37,22 +37,14 @@
     pl.semaphore_wait(barrier, len(peers))
 
 
-def gather_kernel(w_ref, out_ref, send, recv):
+def gather_steps(w_ref, out_ref, send, recv):
     c, z, y, x = place()
     e = lax.axis_index(EXP)
+    copy = copier(send, recv)
 
     def dev(zz, yy, xx):
         return (zz * 16 + ((yy + 4) % 4) * 4 + (xx + 4) % 4, e)
 
-    def copy(n, src, dst, to):
-        cp = pltpu.make_async_remote_copy(
-            src_ref=src, dst_ref=dst, send_sem=send.at[n], recv_sem=recv.at[n],
-            device_id=to, device_id_type=MESH,
-        )
-        cp.start()
-        return cp
-
-    greet([dev(1 - z, y, x), dev(z, y + 1, x), dev(z, y - 1, x), dev(z, y, x + 1), dev(z, y, x - 1)])
     rows = (pl.ds(0, 48), pl.ds(48, 48))
     copies = []
     first = []
@@ -74,6 +66,7 @@
         down = dev(z, y, x - 1) if along_x else dev(z, y - 1, x)
         return me, (me + 3) % 4, (me + 1) % 4, up, down
 
+    yield
     for phase in (1, 2):
         direct = []
         for h in range(2):
@@ -86,6 +79,7 @@
                 copy(n, view(h, phase, both, me), view(h, phase, both, me), up),
                 copy(n + 1, view(h, phase, both, me), view(h, phase, both, me), down),
             ))
+        yield
         later = []
         for h in range(2):
             me, low, high, up, down = ring(h, phase)
@@ -98,6 +92,7 @@
         for h in range(2):
             copies += [*direct[h], *later[h]]
         first = later
+        yield
     for h in range(2):
         for cp in first[h]:
             cp.wait_recv()
@@ -105,17 +100,50 @@
         cp.wait_send()
 
 
-def gather_weights(shard):
-    out = pl.pallas_call(
+def near_peers():
+    c, z, y, x = place()
+    e = lax.axis_index(EXP)
+    return [
+        ((1 - z) * 16 + y * 4 + x, e),
+        (z * 16 + (y + 1) % 4 * 4 + x, e),
+        (z * 16 + (y + 3) % 4 * 4 + x, e),
+        (z * 16 + y * 4 + (x + 1) % 4, e),
+        (z * 16 + y * 4 + (x + 3) % 4, e),
+    ]
+
+
+def pad_into(ref, values):
+    ref[...] = jnp.zeros_like(ref)
+    for i in range(32):
+        ref[:, PADDED * i : PADDED * i + SHARD] = values[:, SHARD * i : SHARD * (i + 1)]
+
+
+def gather_kernel(qkv_ref, o_ref, tokens, full_qkv, full_o, normed_pad, s0, r0, s1, r1):
+    greet(near_peers())
+    first, second = gather_steps(qkv_ref, full_qkv, s0, r0), gather_steps(o_ref, full_o, s1, r1)
+    next(first)
+    next(second)
+    values = f32(tokens[...])
+    pad_into(normed_pad, bf(values * inverse_rms(values)))
+    take_turns(first, second)
+
+
+def gather_weights(qkv, out, tokens):
+    b = jnp.bfloat16
+    full_qkv, full_o, normed_pad = pl.pallas_call(
         gather_kernel,
-        out_shape=jax.ShapeDtypeStruct((2, 4, 4, PADDED, 640), jnp.bfloat16),
-        in_specs=vmem_specs(1),
-        out_specs=vmem_specs(1)[0],
-        scratch_shapes=[pltpu.SemaphoreType.DMA((18,)), pltpu.SemaphoreType.DMA((18,))],
+        out_shape=[
+            jax.ShapeDtypeStruct((2, 4, 4, PADDED, 384), b),
+            jax.ShapeDtypeStruct((2, 4, 4, PADDED, 256), b),
+            jax.ShapeDtypeStruct((128, 32 * PADDED), b),
+        ],
+        in_specs=vmem_specs(3),
+        out_specs=vmem_specs(3),
+        scratch_shapes=[pltpu.SemaphoreType.DMA((18,))] * 4,
         compiler_params=params(0),
         name="gather_weights",
-    )(shard)
-    return out.reshape(32 * PADDED, 640)
+    )(qkv, out, tokens)
+    return full_qkv.reshape(32 * PADDED, 384), full_o.reshape(32 * PADDED, 256), normed_pad
 
 
 def f32(v):
@@ -216,18 +244,18 @@
         cp.wait_send()
 
 
-def scatter_scratch():
+def scatter_scratch(width):
     b = jnp.bfloat16
     return [
-        pltpu.VMEM((2, 2, 4, 48, 640), b),
-        pltpu.VMEM((2, 2, 2, 4, 48, 640), b),
-        pltpu.VMEM((2, 2, 4, 48, 640), b),
-        pltpu.VMEM((2, 2, 4, 48, 640), b),
-        pltpu.VMEM((2, 2, 48, 640), b),
-        pltpu.VMEM((2, 2, 2, 48, 640), b),
-        pltpu.VMEM((2, 2, 48, 640), b),
-        pltpu.VMEM((2, 2, 48, 640), b),
-        pltpu.VMEM((2, 48, 640), b),
+        pltpu.VMEM((2, 2, 4, 48, width), b),
+        pltpu.VMEM((2, 2, 2, 4, 48, width), b),
+        pltpu.VMEM((2, 2, 4, 48, width), b),
+        pltpu.VMEM((2, 2, 4, 48, width), b),
+        pltpu.VMEM((2, 2, 48, width), b),
+        pltpu.VMEM((2, 2, 2, 48, width), b),
+        pltpu.VMEM((2, 2, 48, width), b),
+        pltpu.VMEM((2, 2, 48, width), b),
+        pltpu.VMEM((2, 48, width), b),
         pltpu.SemaphoreType.DMA((26,)),
         pltpu.SemaphoreType.DMA((26,)),
     ]
@@ -326,12 +354,12 @@
 
 
 def attention_kernel(
-    normed_pad, full, tokens, residual, projected, span, attended, prob_ref, part, rim_send, rim_recv, *scratch
+    normed_pad, full_qkv, full_o, tokens, residual, projected, span, attended, prob_ref, part, rim_send, rim_recv, *scratch
 ):
     c = lax.axis_index(CTX)
     after, before = ring_ctx()
     greet([*exp_peers(), after, before])
-    made = bf(dot(normed_pad[...], full[:, :384]))
+    made = bf(dot(normed_pad[...], full_qkv[...]))
     projected[...] = made
     span[128:, :] = made[:, 256:]
     rim = copier(rim_send, rim_recv)(0, span.at[pl.ds(128, 128)], span.at[pl.ds(0, 128)], after)
@@ -345,12 +373,12 @@
         prob = weights / jnp.sum(weights, axis=-1, keepdims=True)
         prob_ref[h] = prob
         attended[:, HEAD_SIZE * h : HEAD_SIZE * (h + 1)] = bf(dot(bf(prob), values))
-    drop_into(part, bf(dot_nt(attended[...], full[:, 384:])))
+    drop_into(part, bf(dot_nt(attended[...], full_o[...])))
     rim.wait_send()
     take_turns(sum_steps(lambda t, m: add_base(t, m, tokens), part, residual, *scratch))
 
 
-def attention(normed_pad, full, tokens):
+def attention(normed_pad, full_qkv, full_o, tokens):
     b = jnp.bfloat16
     shape = jax.ShapeDtypeStruct
     return pl.pallas_call(
@@ -359,59 +387,45 @@
             shape((128, MODEL), b), shape((128, 384), b), shape((256, 128), b), shape((128, 256), b),
             shape((4, 128, 256), jnp.float32),
         ],
-        in_specs=vmem_specs(3),
+        in_specs=vmem_specs(4),
         out_specs=vmem_specs(5),
         scratch_shapes=[
             pltpu.VMEM((128, MODEL), b), pltpu.SemaphoreType.DMA((1,)), pltpu.SemaphoreType.DMA((1,)),
         ] + sum_scratch(),
         compiler_params=params(1),
         name="attention",
-    )(normed_pad, full, tokens)
-
-
-def grad_residual_kernel(part, cotangent, residual, out, own, *scratch):
-    greet(exp_peers())
-    take_turns(sum_steps(lambda t, m: finish_resid(t, m, cotangent, residual, own), part, out, *scratch))
-
-
-def grad_residual(part, cotangent, residual):
-    return pl.pallas_call(
-        grad_residual_kernel,
-        out_shape=[
-            jax.ShapeDtypeStruct((128, MODEL), jnp.bfloat16),
-            jax.ShapeDtypeStruct((16, MODEL), jnp.float32),
-        ],
-        in_specs=vmem_specs(3),
-        out_specs=vmem_specs(2),
-        scratch_shapes=sum_scratch(),
-        compiler_params=params(3),
-        name="grad_residual",
-    )(part, cotangent, residual)
+    )(normed_pad, full_qkv, full_o, tokens)
 
 
 def last_kernel(
-    moe_part, residual, tokens, grad_resid, grad_resid_bf, normed_pad, full, projected, span, attended, prob_ref,
-    block_out, grad_tokens, sums,
-    resid_pad, qkv_grad, rim_out, rim_in, grad_part, terms, rim_send, rim_recv, *scratch
+    grad_in_part, moe_part, cotangent, residual, tokens, normed_pad, full_qkv, full_o, projected, span, attended, prob_ref,
+    block_out, grad_tokens, sum_qkv, sum_o,
+    grad_resid_bf, grad_resid, resid_pad, qkv_grad, rim_out, rim_in, grad_part, terms_qkv, terms_o,
+    rim_send, rim_recv, *scratch
 ):
-    c, z, y, x = place()
-    e = lax.axis_index(EXP)
     after, before = ring_ctx()
-    near = [
-        ((1 - z) * 16 + y * 4 + x, e),
-        (z * 16 + (y + 1) % 4 * 4 + x, e),
-        (z * 16 + (y + 3) % 4 * 4 + x, e),
-        (z * 16 + y * 4 + (x + 1) % 4, e),
-        (z * 16 + y * 4 + (x + 3) % 4, e),
-    ]
-    greet([*near, *exp_peers(), after, before])
-    block_sum = sum_steps(lambda t, m: add_base(t, m, residual), moe_part, block_out, *scratch[6:12])
-    next(block_sum)
-
-    resid_pad[...] = jnp.zeros_like(resid_pad)
-    for i in range(32):
-        resid_pad[:, PADDED * i : PADDED * i + SHARD] = grad_resid_bf[:, SHARD * i : SHARD * (i + 1)]
-    attended_grad = bf(dot(resid_pad[...], full[:, 384:]))
+    greet([*near_peers(), *exp_peers(), after, before])
+    take_turns(
+        sum_steps(
+            lambda t, m: finish_resid(t, m, cotangent, residual, grad_resid), grad_in_part, grad_resid_bf, *scratch[:6]
+        ),
+        sum_steps(lambda t, m: add_base(t, m, residual), moe_part, block_out, *scratch[6:12]),
+    )
+
+    def term(left, right, terms):
+        def four(i, t):
+            rows = left[:, pl.ds(pl.multiple_of(i * 384, 128), 384)]
+            terms[i // 4, i % 4] = bf(dot_tn(rows, right)).reshape(4, PADDED, right.shape[1])
+            return t
+
+        lax.fori_loop(0, 8, four, 0)
+
+    pad_into(resid_pad, grad_resid_bf[...])
+    term(resid_pad, attended[...], terms_o)
+    output_sum = scatter_steps(terms_o, sum_o, *scratch[18:29])
+    next(output_sum)
+
+    attended_grad = bf(dot(resid_pad[...], full_o[...]))
     keys, values = span[:, :HEAD_SIZE], span[:, HEAD_SIZE:]
     grad_key = jnp.zeros((256, HEAD_SIZE), jnp.float32)
     grad_value = jnp.zeros((256, HEAD_SIZE), jnp.float32)
@@ -429,49 +443,41 @@
     rim_out[:, HEAD_SIZE:] = bf(grad_value[:128])
     rim = copier(rim_send, rim_recv)(0, rim_out, rim_in, before)
 
-    def term(left, right, columns):
-        def four(i, t):
-            rows = left[:, pl.ds(pl.multiple_of(i * 384, 128), 384)]
-            terms[i // 4, i % 4, :, :, columns] = bf(dot_tn(rows, right)).reshape(4, PADDED, columns.size)
-            return t
-
-        lax.fori_loop(0, 8, four, 0)
-
-    term(resid_pad, attended[...], pl.ds(384, 256))
-    next(block_sum)
+    next(output_sum)
     rim.wait()
     qkv_grad[:, 256:320] = bf(grad_key[128:] + f32(rim_in[:, :HEAD_SIZE]))
     qkv_grad[:, 320:] = bf(grad_value[128:] + f32(rim_in[:, HEAD_SIZE:]))
     grads = qkv_grad[...]
-    drop_into(grad_part, bf(dot_nt(grads, full[:, :384])))
+    drop_into(grad_part, bf(dot_nt(grads, full_qkv[...])))
     token_sum = sum_steps(
-        lambda t, m: finish_tokens(t, m, tokens, grad_resid), grad_part, grad_tokens, *scratch[:6]
+        lambda t, m: finish_tokens(t, m, tokens, grad_resid), grad_part, grad_tokens, *scratch[12:18]
     )
     next(token_sum)
-    term(normed_pad, grads, pl.ds(0, 384))
-    take_turns(scatter_steps(terms, sums, *scratch[12:]), token_sum, block_sum)
+    term(normed_pad, grads, terms_qkv)
+    take_turns(scatter_steps(terms_qkv, sum_qkv, *scratch[29:]), output_sum, token_sum)
 
 
 def last_sums(*operands):
     b = jnp.bfloat16
+    shape = jax.ShapeDtypeStruct
     return pl.pallas_call(
         last_kernel,
-        out_shape=[
-            jax.ShapeDtypeStruct((128, MODEL), b), jax.ShapeDtypeStruct((128, MODEL), b),
-            jax.ShapeDtypeStruct((PADDED, 640), b),
-        ],
-        in_specs=vmem_specs(11),
-        out_specs=vmem_specs(3),
+        out_shape=[shape((128, MODEL), b), shape((128, MODEL), b), shape((PADDED, 384), b), shape((PADDED, 256), b)],
+        in_specs=vmem_specs(12),
+        out_specs=vmem_specs(4),
         scratch_shapes=[
+            pltpu.VMEM((128, MODEL), b),
+            pltpu.VMEM((16, MODEL), jnp.float32),
             pltpu.VMEM((128, 32 * PADDED), b),
             pltpu.VMEM((128, 384), b),
             pltpu.VMEM((128, 128), b),
             pltpu.VMEM((128, 128), b),
             pltpu.VMEM((128, MODEL), b),
-            pltpu.VMEM((2, 4, 4, PADDED, 640), b),
+            pltpu.VMEM((2, 4, 4, PADDED, 384), b),
+            pltpu.VMEM((2, 4, 4, PADDED, 256), b),
             pltpu.SemaphoreType.DMA((1,)),
             pltpu.SemaphoreType.DMA((1,)),
-        ] + sum_scratch() + sum_scratch() + scatter_scratch(),
+        ] + sum_scratch() * 3 + scatter_scratch(256) + scatter_scratch(384),
         compiler_params=params(4),
         name="last_sums",
     )(*operands)
@@ -506,10 +512,6 @@
 def rms_back(values, inv_rms, grad_in):
     inner_mean = jnp.mean(grad_in * values, axis=-1, keepdims=True)
     return inv_rms * grad_in - values * (inv_rms * inv_rms * inv_rms) * inner_mean
-
-
-def pad_features(v):
-    return jnp.pad(v.reshape(-1, 32, SHARD), ((0, 0), (0, 0), (0, PADDED - SHARD))).reshape(-1, 32 * PADDED)
 
 
 def iota(shape, axis):
@@ -838,23 +840,19 @@
     tokens, cotangent, expert_ids, combine_weights,
     w_query, key_value_weight, w_output, w_gate, w_up, w_down,
 ):
-    tokens_f32 = f32(tokens)
-    normed = bf(tokens_f32 * inverse_rms(tokens_f32))
-    normed_pad = pad_features(normed)
-    shard = jnp.concatenate([w_query, key_value_weight, w_output.T], axis=1)
-    full = gather_weights(jnp.pad(shard, ((0, PADDED - SHARD), (0, 0))))
-
-    residual, projected, span, attended, prob = attention(normed_pad, full, tokens)
+    widen = lambda v: jnp.pad(v, ((0, PADDED - SHARD), (0, 0)))
+    full_qkv, full_o, normed_pad = gather_weights(
+        widen(jnp.concatenate([w_query, key_value_weight], axis=1)), widen(w_output.T), tokens
+    )
+    residual, projected, span, attended, prob = attention(normed_pad, full_qkv, full_o, tokens)
     grad_in_part, moe_part, grad_gate, grad_up, grad_down = experts(
         residual, cotangent, expert_ids, combine_weights, w_gate[0], w_up[0], w_down[0]
     )
-    grad_resid_bf, grad_resid = grad_residual(grad_in_part, cotangent, residual)
-    block_out, grad_tokens, sums = last_sums(
-        moe_part, residual, tokens, grad_resid, grad_resid_bf, normed_pad, full, projected, span, attended, prob
+    block_out, grad_tokens, sum_qkv, sum_o = last_sums(
+        grad_in_part, moe_part, cotangent, residual, tokens, normed_pad, full_qkv, full_o, projected, span, attended, prob
     )
-    sums = sums[:SHARD]
     return (
-        block_out, grad_tokens, sums[:, :256], sums[:, 256:384], sums[:, 384:].T,
+        block_out, grad_tokens, sum_qkv[:SHARD, :256], sum_qkv[:SHARD, 256:], sum_o[:SHARD].T,
         grad_gate[None], grad_up[None], grad_down[None],
     )
 

time: 317 us -> 320 us (level)
    pallas_call x3 -> x2, Pallas kernels: 118 us -> 122 us  [the longest x1 89.2 us: last_sums(): pl.pallas_call(last_kernel, out_shape=[shape((128, MODEL), b), shape((128...]
where the time goes in v4:
time: 320 us; the launch traced here: 318 us
  Pallas kernels  296 us (92%)
  local copies, waits for them, and re-layouts  19.5 us (6%)
    pallas_call x1, Pallas kernels, experts(): pl.pallas_call(expert_kernel, out_shape=[shape((128, MODEL), b), shape((1...  131 us
    pallas_call x1, Pallas kernels, last_sums(): pl.pallas_call(last_kernel, out_shape=[shape((128, MODEL), b), shape((128...  89.2 us
    pallas_call x1, Pallas kernels, attention(): pl.pallas_call(attention_kernel, out_shape=[shape((128, MODEL), b), shape...  43.5 us
    pallas_call x1, Pallas kernels, gather_weights(): pl.pallas_call(gather_kernel, out_shape=[jax.ShapeDtypeStruct((2, 4, 4, P...  32.8 us
    unnamed x26, local copies, waits for them, and re-layouts  16.2 us

profile of v4, /device:TPU:1, one launch (start us, length us, event | category | flops | bytes accessed | tf_op | source)
XLA Modules:
  0.0 318.0 jit_solution(11874862718624580437)
XLA Ops:
  0.6 0.0 copy-start.5
  0.6 1.5 pad.9.o_ref
  2.1 1.4 copy.22.ids_ref
  3.6 1.4 copy.23.combine_ref
  5.0 1.5 fusion.2.qkv_ref
  6.4 2.4 copy.18.tokens
  8.8 0.0 copy-done.5
  8.8 1.2 copy.21.cot_ref.cotangent
  10.0 0.0 copy-done.1
  10.0 1.7 copy.20
  11.7 32.8 %gather_weights.1 = (bf16[2,4,4,96,384]{4,3,2,1,0:T(8,128)(2,1)}, bf16[2,4,4,96,256]{4,3,2,1,0:T(8,128)(2,1)}, bf16[128,3072]{1,0:T(8,128)(2,1)}) custom-call(bf16[96,384]{1,0:T(8,128)(2,1)} %fusion.2.qkv_ref, bf16[96,256]{1,0:T(8,128)(2,1)} %pad.9.o_ref, bf16[128,2880]{1,0:T(8,128)(2,1)} %copy.18.tokens), custom_call_target="tpu_custom_call" | custom-call | tf_op jit(solution)/shard_map/gather_weights/pallas_call | solution.py:133
  44.4 43.5 %attention.1 = (bf16[128,2880]{1,0:T(8,128)(2,1)}, bf16[128,384]{1,0:T(8,128)(2,1)}, bf16[256,128]{1,0:T(8,128)(2,1)}, bf16[128,256]{1,0:T(8,128)(2,1)}, f32[4,128,256]{2,1,0:T(8,128)}) custom-call(bf16[128,3072]{1,0:T(8,128)(2,1)} %get-tuple-element.25.normed_pad, bf16[3072,384]{1,0:T(8,128)(2,1)} %bitcast.11, bf16[3072,256]{1,0:T(8,128)(2,1)} %bitcast.13, ...), custom_call_target="tpu_custom_call" | custom-call | tf_op jit(solution)/shard_map/attention/pallas_call | solution.py:384
  87.9 130.7 %experts.1 = (bf16[128,2880]{1,0:T(8,128)(2,1)}, bf16[128,2880]{1,0:T(8,128)(2,1)}, bf16[2880,256]{1,0:T(8,128)(2,1)}, bf16[2880,256]{1,0:T(8,128)(2,1)}, bf16[256,2880]{1,0:T(8,128)(2,1)}) custom-call(bf16[128,2880]{1,0:T(8,128)(2,1)} %get-tuple-element.28.x_ref.residual, bf16[128,2880]{1,0:T(8,128)(2,1)} %copy.21.cot_ref.cotangent, ...), custom_call_target="tpu_custom_call" | custom-call | tf_op jit(solution)/shard_map/experts/pallas_call | solution.py:791
  218.7 89.2 %last_sums.1 = (bf16[128,2880]{1,0:T(8,128)(2,1)}, bf16[128,2880]{1,0:T(8,128)(2,1)}, bf16[96,384]{1,0:T(8,128)(2,1)}, bf16[96,256]{1,0:T(8,128)(2,1)}) custom-call(bf16[128,2880]{1,0:T(8,128)(2,1)} %get-tuple-element.29.grad_in_part, bf16[128,2880]{1,0:T(8,128)(2,1)} %get-tuple-element.30.moe_part, bf16[128,2880]{1,0:T(8,128)(2,1)} %copy.21.cot_ref.cotangent, ...), custom_call_target="tpu_custom_call" | custom-call | tf_op jit(solution)/shard_map/last_sums/pallas_call | solution.py:463
  308.0 2.4 copy.26
  310.4 0.6 slice.10
  311.0 0.6 slice.9
  311.6 0.6 slice_bitcast_fusion
  312.3 1.1 copy.27
  313.4 1.5 copy.28
  314.9 0.0 copy-done.3
  314.9 1.1 copy.31
  316.1 0.8 copy-done.2
  316.9 1.1 copy.32
  (11 shorter events, 0.0 us)
Async XLA Ops:
  0.6 8.2 %copy-start.5 = (bf16[128,2880]{0,1:T(8,128)(2,1)S(1)}, bf16[128,2880]{0,1:T(8,128)(2,1)}, u32[]{:S(2)}) copy-start(bf16[128,2880]{0,1:T(8,128)(2,1)} %param.11) | copy-start | bytes 2211844
  6.4 3.5 %copy-start.1 = (bf16[1,256,2880]{1,2,0:T(8,128)(2,1)S(1)}, bf16[1,256,2880]{1,2,0:T(8,128)(2,1)}, u32[]{:S(2)}) copy-start(bf16[1,256,2880]{1,2,0:T(8,128)(2,1)} %param.19) | copy-start | bytes 4423684
  307.9 2.5 copy-start.6
  307.9 3.7 %copy-start.7 = (bf16[96,256]{1,0:T(8,128)(2,1)S(1)}, bf16[96,256]{1,0:T(8,128)(2,1)}, u32[]{:S(2)}) copy-start(bf16[96,256]{1,0:T(8,128)(2,1)} %get-tuple-element.38) | copy-start | bytes 147460
  308.0 4.3 %copy-start.4 = (bf16[128,2880]{1,0:T(8,128)(2,1)S(1)}, bf16[128,2880]{1,0:T(8,128)(2,1)}, u32[]{:S(2)}) copy-start(bf16[128,2880]{1,0:T(8,128)(2,1)} %get-tuple-element.43) | copy-start | bytes 2211844
  308.0 5.4 %copy-start = (bf16[256,2880]{1,0:T(8,128)(2,1)S(1)}, bf16[256,2880]{1,0:T(8,128)(2,1)}, u32[]{:S(2)}) copy-start(bf16[256,2880]{1,0:T(8,128)(2,1)} %get-tuple-element.41) | copy-start | bytes 4423684
  313.4 1.5 copy-start.3
  314.9 1.9 copy-start.2
